TPU v7x, 32 devices: a whole 2x2x4 slice. The times are simulated.
32 devices in a mesh: fsdp: 2 (over x), ctx: 4 (over y, core), tp: 4 (over z).
Axes of the slice: x: 2, y: 2, z: 4, core: 2. Of those that a mesh axis runs over, the one named last changes fastest.
Arguments:
- tokens: bfloat16 [12288, 768], P(('fsdp', 'ctx')), may hold values from -6 to 6
- cotangent: bfloat16 [12288, 768], P(('fsdp', 'ctx')), may hold values from -6 to 6
- doc_lengths: int32 [2, 3], P('fsdp'), may hold values from 1 to 5376, 6144 in all within a row
- ln1_gain: bfloat16 [768], P('fsdp'), may hold values from 0.099609375 to 1.8984375
- ln1_bias: bfloat16 [768], P('fsdp'), may hold values from -4 to 4
- ln2_gain: bfloat16 [768], P('fsdp'), may hold values from 0.099609375 to 1.8984375
- ln2_bias: bfloat16 [768], P('fsdp'), may hold values from -4 to 4
- w_qkv: bfloat16 [3, 768, 768], P(None, 'fsdp', 'tp'), may hold values from -0.21875 to 0.21875
- qv_bias: bfloat16 [2, 768], P(None, ('tp', 'fsdp')), may hold values from -6 to 6
- w_out: bfloat16 [768, 768], P('tp', 'fsdp'), may hold values from -1.75 to 1.75
- out_bias: bfloat16 [768], P('fsdp'), may hold values from -4 to 4
- w_in: bfloat16 [768, 3072], P('fsdp', 'tp'), may hold values from -0.21875 to 0.21875
- in_bias: bfloat16 [3072], P(('tp', 'fsdp')), may hold values from -6 to 6
- w_back: bfloat16 [3072, 768], P('tp', 'fsdp'), may hold values from -0.109375 to 0.109375
- back_bias: bfloat16 [768], P('fsdp'), may hold values from -4 to 4
Outputs:
- mixed: bfloat16 [12288, 768], P(('fsdp', 'ctx'))
- input_grad: float32 [12288, 768], P(('fsdp', 'ctx'))
- ln1_gain_grad: float32 [768], P('fsdp')
- ln1_bias_grad: float32 [768], P('fsdp')
- ln2_gain_grad: float32 [768], P('fsdp')
- ln2_bias_grad: float32 [768], P('fsdp')
- w_qkv_grad: float32 [3, 768, 768], P(None, 'fsdp', 'tp')
- qv_bias_grad: float32 [2, 768], P(None, ('tp', 'fsdp'))
- w_out_grad: float32 [768, 768], P('tp', 'fsdp')
- out_bias_grad: float32 [768], P('fsdp')
- w_in_grad: float32 [768, 3072], P('fsdp', 'tp')
- in_bias_grad: float32 [3072], P(('tp', 'fsdp'))
- w_back_grad: float32 [3072, 768], P('tp', 'fsdp')
- back_bias_grad: float32 [768], P('fsdp')
Inputs may be any that keep to these rules, and one draw needn't show every extreme that they name: `doc_lengths`: row g lists the lengths of the documents packed in order into group g's 6144 tokens; each row sums to 6144 and its largest entry is 5376.
All inputs are finite; a program needn't handle non-finite values.
Results may differ from a plain program's by a relative error of at most 0.023.
Values may be sent and summed in bfloat16 or wider, within the bound.
A program may use at most 128 MiB of HBM per device.

v0:
```python
import jax
import jax.numpy as jnp
from jax import lax
from jax.sharding import PartitionSpec as P

HEAD = 64


norm_epsilon = 1e-05
masked_score = -1e30


def layer_norm(inputs_f, norm_gain, norm_shift):
    centred = inputs_f - jnp.mean(inputs_f, axis=-1, keepdims=True)
    spread = jnp.mean(centred * centred, axis=-1, keepdims=True)
    return centred * lax.rsqrt(spread + norm_epsilon) * norm_gain + norm_shift


def smooth_act(inputs_f):
    return jax.nn.gelu(inputs_f, approximate=True)


def mat_product(left_side, right_side):
    return jnp.dot(left_side, right_side, preferred_element_type=jnp.float32)


def left_product(left_side, right_side):
    return lax.dot_general(
        left_side, right_side, (((0,), (0,)), ((), ())), preferred_element_type=jnp.float32
    )


def right_product(left_side, right_side):
    return lax.dot_general(
        left_side, right_side, (((1,), (1,)), ((), ())), preferred_element_type=jnp.float32
    )


def doc_numbers(positions, bounds):
    return jnp.sum((positions[:, None] >= bounds[None, :]).astype(jnp.int32), axis=1)


def column_sums(matrix):
    return jnp.sum(matrix.astype(jnp.float32), axis=0)


def on_device(
    tokens,
    cotangent,
    doc_lengths,
    ln1_gain,
    ln1_bias,
    ln2_gain,
    ln2_bias,
    w_qkv,
    qv_bias,
    w_out,
    out_bias,
    w_in,
    in_bias,
    w_back,
    back_bias,
):
    rows_here = tokens.shape[0]
    ctx_size = lax.axis_size("ctx")
    ctx_place = lax.axis_index("ctx")
    (
        gain_one,
        shift_one,
        gain_two,
        shift_two,
        qkv_full,
        qv_full,
        out_full,
        out_shift,
        in_full,
        in_shift,
        back_full,
        back_shift,
    ) = (
        lax.all_gather(ln1_gain, "fsdp", axis=0, tiled=True),
        lax.all_gather(ln1_bias, "fsdp", axis=0, tiled=True),
        lax.all_gather(ln2_gain, "fsdp", axis=0, tiled=True),
        lax.all_gather(ln2_bias, "fsdp", axis=0, tiled=True),
        lax.all_gather(w_qkv, "fsdp", axis=1, tiled=True),
        lax.all_gather(qv_bias, "fsdp", axis=1, tiled=True),
        lax.all_gather(w_out, "fsdp", axis=1, tiled=True),
        lax.all_gather(out_bias, "fsdp", axis=0, tiled=True),
        lax.all_gather(w_in, "fsdp", axis=0, tiled=True),
        lax.all_gather(in_bias, "fsdp", axis=0, tiled=True),
        lax.all_gather(w_back, "fsdp", axis=1, tiled=True),
        lax.all_gather(back_bias, "fsdp", axis=0, tiled=True),
    )
    gain_one = gain_one.astype(jnp.float32)
    shift_one = shift_one.astype(jnp.float32)
    gain_two = gain_two.astype(jnp.float32)
    shift_two = shift_two.astype(jnp.float32)
    qv_float = qv_full.astype(jnp.float32)
    out_shift = out_shift.astype(jnp.float32)
    in_shift = in_shift.astype(jnp.float32)
    back_shift = back_shift.astype(jnp.float32)
    local_width = qkv_full.shape[2]
    local_heads = local_width // HEAD
    score_scale = HEAD ** (-0.5)
    tokens_f = tokens.astype(jnp.float32)
    cot_f = cotangent.astype(jnp.float32)
    normed_one = layer_norm(tokens_f, gain_one, shift_one).astype(jnp.bfloat16)
    queries = (mat_product(normed_one, qkv_full[0]) + qv_float[0]).astype(jnp.bfloat16)
    key_rows = mat_product(normed_one, qkv_full[1]).astype(jnp.bfloat16)
    value_rows = (mat_product(normed_one, qkv_full[2]) + qv_float[1]).astype(jnp.bfloat16)
    key_all, value_all = (
        lax.all_gather(key_rows, "ctx", axis=0, tiled=True),
        lax.all_gather(value_rows, "ctx", axis=0, tiled=True),
    )
    bounds = jnp.cumsum(doc_lengths[0])[:-1]
    query_pos = ctx_place * rows_here + jnp.arange(rows_here, dtype=jnp.int32)
    last_query = ctx_place * rows_here + rows_here - 1
    query_doc = doc_numbers(query_pos, bounds)
    block_rows = rows_here // 2
    block_count = 2 * ctx_size
    key_blocks = key_all.reshape(block_count, block_rows, local_heads, HEAD)
    value_blocks = value_all.reshape(block_count, block_rows, local_heads, HEAD)
    block_starts = jnp.arange(block_count, dtype=jnp.int32) * block_rows
    query_heads = queries.reshape(rows_here, local_heads, HEAD)

    def block_scores(key_block, block_start):
        key_pos = block_start + jnp.arange(block_rows, dtype=jnp.int32)
        allowed = (query_doc[:, None] == doc_numbers(key_pos, bounds)[None, :]) & (
            key_pos[None, :] <= query_pos[:, None]
        )
        raw_scores = (
            jnp.einsum("qhd,khd->hqk", query_heads, key_block, preferred_element_type=jnp.float32)
            * score_scale
        )
        return jnp.where(allowed[None], raw_scores, masked_score)

    def attend(carry, block_item):
        key_block, value_block, block_start = block_item

        def visit(state):
            running_max, running_sum, running_out = state
            scores = block_scores(key_block, block_start)
            new_max = jnp.maximum(running_max, jnp.max(scores, axis=2, keepdims=True))
            rescale = jnp.exp(running_max - new_max)
            unnormed = jnp.exp(scores - new_max)
            new_sum = running_sum * rescale + jnp.sum(unnormed, axis=2, keepdims=True)
            new_out = running_out * rescale + jnp.einsum(
                "hqk,khd->hqd",
                unnormed.astype(jnp.bfloat16),
                value_block,
                preferred_element_type=jnp.float32,
            )
            return (new_max, new_sum, new_out)

        def leave(state):
            return state

        return (lax.cond(block_start <= last_query, visit, leave, carry), None)

    start_state = (
        jnp.full((local_heads, rows_here, 1), masked_score, jnp.float32),
        jnp.zeros((local_heads, rows_here, 1), jnp.float32),
        jnp.zeros((local_heads, rows_here, HEAD), jnp.float32),
    )
    (final_max, final_sum, final_out), unused = lax.scan(
        attend, start_state, (key_blocks, value_blocks, block_starts)
    )
    log_total = final_max + jnp.log(final_sum)
    attn_out = final_out / final_sum
    attended = attn_out.transpose(1, 0, 2).reshape(rows_here, local_width).astype(jnp.bfloat16)
    attn_partial = mat_product(attended, out_full)
    residual = (
        tokens_f + lax.psum(attn_partial.astype(jnp.bfloat16), "tp").astype(jnp.float32) + out_shift
    )
    normed_two = layer_norm(residual, gain_two, shift_two).astype(jnp.bfloat16)
    hidden = mat_product(normed_two, in_full) + in_shift
    active = smooth_act(hidden).astype(jnp.bfloat16)
    ff_partial = mat_product(active, back_full)
    mixed = (
        residual + lax.psum(ff_partial.astype(jnp.bfloat16), "tp").astype(jnp.float32) + back_shift
    ).astype(jnp.bfloat16)
    back_shift_grad = column_sums(cotangent)
    back_grad = left_product(active, cotangent)
    grad_active = right_product(cotangent, back_full)
    unused, gelu_pull = jax.vjp(smooth_act, hidden)
    grad_hidden = gelu_pull(grad_active)[0].astype(jnp.bfloat16)
    in_shift_grad = column_sums(grad_hidden)
    in_grad = left_product(normed_two, grad_hidden)
    norm_two_partial = right_product(grad_hidden, in_full)
    grad_normed_two = lax.psum(norm_two_partial.astype(jnp.bfloat16), "tp").astype(jnp.float32)
    unused, second_pull = jax.vjp(layer_norm, residual, gain_two, shift_two)
    grad_residual, gain_two_grad, shift_two_grad = second_pull(grad_normed_two)
    grad_residual = cot_f + grad_residual
    grad_attn = grad_residual.astype(jnp.bfloat16)
    out_shift_grad = column_sums(grad_attn)
    out_grad = left_product(attended, grad_attn)
    grad_attended = right_product(grad_attn, out_full).astype(jnp.bfloat16)
    grad_heads = grad_attended.reshape(rows_here, local_heads, HEAD)
    row_delta = jnp.einsum("qhd,hqd->hq", grad_heads.astype(jnp.float32), attn_out)[:, :, None]
    zero_terms = jnp.zeros((block_rows, local_heads, HEAD), jnp.float32)

    def attend_back(grad_query, block_item):
        key_block, value_block, block_start = block_item

        def visit(grad_now):
            attention = jnp.exp(block_scores(key_block, block_start) - log_total)
            grad_probs = jnp.einsum(
                "qhd,khd->hqk", grad_heads, value_block, preferred_element_type=jnp.float32
            )
            grad_scores = (attention * (grad_probs - row_delta)).astype(jnp.bfloat16)
            grad_next = grad_now + jnp.einsum(
                "hqk,khd->qhd", grad_scores, key_block, preferred_element_type=jnp.float32
            )
            grad_key = jnp.einsum(
                "hqk,qhd->khd", grad_scores, query_heads, preferred_element_type=jnp.float32
            )
            grad_value = jnp.einsum(
                "hqk,qhd->khd",
                attention.astype(jnp.bfloat16),
                grad_heads,
                preferred_element_type=jnp.float32,
            )
            return (grad_next, (grad_key, grad_value))

        def leave(grad_now):
            return (grad_now, (zero_terms, zero_terms))

        return lax.cond(block_start <= last_query, visit, leave, grad_query)

    grad_query_sum, (key_terms, value_terms) = lax.scan(
        attend_back,
        jnp.zeros((rows_here, local_heads, HEAD), jnp.float32),
        (key_blocks, value_blocks, block_starts),
    )
    key_sum, value_sum = (
        lax.psum_scatter(
            key_terms.reshape(block_count * block_rows, local_width).astype(jnp.bfloat16),
            "ctx",
            scatter_dimension=0,
            tiled=True,
        ).astype(jnp.float32),
        lax.psum_scatter(
            value_terms.reshape(block_count * block_rows, local_width).astype(jnp.bfloat16),
            "ctx",
            scatter_dimension=0,
            tiled=True,
        ).astype(jnp.float32),
    )
    grad_keys = (key_sum * score_scale).astype(jnp.bfloat16)
    grad_values = value_sum.astype(jnp.bfloat16)
    grad_queries = (
        (grad_query_sum * score_scale).reshape(rows_here, local_width).astype(jnp.bfloat16)
    )
    qkv_grad = jnp.stack(
        [
            left_product(normed_one, grad_queries),
            left_product(normed_one, grad_keys),
            left_product(normed_one, grad_values),
        ]
    )
    qv_grad = jnp.stack([column_sums(grad_queries), column_sums(grad_values)])
    norm_one_partial = (
        right_product(grad_queries, qkv_full[0])
        + right_product(grad_keys, qkv_full[1])
        + right_product(grad_values, qkv_full[2])
    )
    grad_normed_one = lax.psum(norm_one_partial.astype(jnp.bfloat16), "tp").astype(jnp.float32)
    unused, first_pull = jax.vjp(layer_norm, tokens_f, gain_one, shift_one)
    grad_tokens, gain_one_grad, shift_one_grad = first_pull(grad_normed_one)
    input_rows = grad_residual + grad_tokens
    (
        part_g1,
        part_s1,
        part_g2,
        part_s2,
        part_qkv,
        part_qv,
        part_out,
        part_ob,
        part_in,
        part_ib,
        part_back,
        part_bb,
    ) = (
        lax.psum_scatter(
            gain_one_grad.astype(jnp.bfloat16), "fsdp", scatter_dimension=0, tiled=True
        ).astype(jnp.float32),
        lax.psum_scatter(
            shift_one_grad.astype(jnp.bfloat16), "fsdp", scatter_dimension=0, tiled=True
        ).astype(jnp.float32),
        lax.psum_scatter(
            gain_two_grad.astype(jnp.bfloat16), "fsdp", scatter_dimension=0, tiled=True
        ).astype(jnp.float32),
        lax.psum_scatter(
            shift_two_grad.astype(jnp.bfloat16), "fsdp", scatter_dimension=0, tiled=True
        ).astype(jnp.float32),
        lax.psum_scatter(
            qkv_grad.astype(jnp.bfloat16), "fsdp", scatter_dimension=1, tiled=True
        ).astype(jnp.float32),
        lax.psum_scatter(
            qv_grad.astype(jnp.bfloat16), "fsdp", scatter_dimension=1, tiled=True
        ).astype(jnp.float32),
        lax.psum_scatter(
            out_grad.astype(jnp.bfloat16), "fsdp", scatter_dimension=1, tiled=True
        ).astype(jnp.float32),
        lax.psum_scatter(
            out_shift_grad.astype(jnp.bfloat16), "fsdp", scatter_dimension=0, tiled=True
        ).astype(jnp.float32),
        lax.psum_scatter(
            in_grad.astype(jnp.bfloat16), "fsdp", scatter_dimension=0, tiled=True
        ).astype(jnp.float32),
        lax.psum_scatter(
            in_shift_grad.astype(jnp.bfloat16), "fsdp", scatter_dimension=0, tiled=True
        ).astype(jnp.float32),
        lax.psum_scatter(
            back_grad.astype(jnp.bfloat16), "fsdp", scatter_dimension=1, tiled=True
        ).astype(jnp.float32),
        lax.psum_scatter(
            back_shift_grad.astype(jnp.bfloat16), "fsdp", scatter_dimension=0, tiled=True
        ).astype(jnp.float32),
    )
    summed = (
        lax.psum(part_g1.astype(jnp.bfloat16), "ctx").astype(jnp.float32),
        lax.psum(part_s1.astype(jnp.bfloat16), "ctx").astype(jnp.float32),
        lax.psum(part_g2.astype(jnp.bfloat16), "ctx").astype(jnp.float32),
        lax.psum(part_s2.astype(jnp.bfloat16), "ctx").astype(jnp.float32),
        lax.psum(part_qkv.astype(jnp.bfloat16), "ctx").astype(jnp.float32),
        lax.psum(part_qv.astype(jnp.bfloat16), "ctx").astype(jnp.float32),
        lax.psum(part_out.astype(jnp.bfloat16), "ctx").astype(jnp.float32),
        lax.psum(part_ob.astype(jnp.bfloat16), "ctx").astype(jnp.float32),
        lax.psum(part_in.astype(jnp.bfloat16), "ctx").astype(jnp.float32),
        lax.psum(part_ib.astype(jnp.bfloat16), "ctx").astype(jnp.float32),
        lax.psum(part_back.astype(jnp.bfloat16), "ctx").astype(jnp.float32),
        lax.psum(part_bb.astype(jnp.bfloat16), "ctx").astype(jnp.float32),
    )
    return (
        mixed,
        input_rows,
        summed[0],
        summed[1],
        summed[2],
        summed[3],
        summed[4],
        summed[5],
        summed[6],
        summed[7],
        summed[8],
        summed[9],
        summed[10],
        summed[11],
    )


def solution(mesh):
    return jax.shard_map(
        on_device,
        mesh=mesh,
        in_specs=(
            P(("fsdp", "ctx"), None),
            P(("fsdp", "ctx"), None),
            P("fsdp", None),
            P("fsdp"),
            P("fsdp"),
            P("fsdp"),
            P("fsdp"),
            P(None, "fsdp", "tp"),
            P(None, ("tp", "fsdp")),
            P("tp", "fsdp"),
            P("fsdp"),
            P("fsdp", "tp"),
            P(("tp", "fsdp")),
            P("tp", "fsdp"),
            P("fsdp"),
        ),
        out_specs=(
            P(("fsdp", "ctx"), None),
            P(("fsdp", "ctx"), None),
            P("fsdp"),
            P("fsdp"),
            P("fsdp"),
            P("fsdp"),
            P(None, "fsdp", "tp"),
            P(None, ("tp", "fsdp")),
            P("tp", "fsdp"),
            P("fsdp"),
            P("fsdp", "tp"),
            P(("tp", "fsdp")),
            P("tp", "fsdp"),
            P("fsdp"),
        ),
        check_vma=False,
    )
```

profile of v0, /device:TPU:0, one launch (start us, length us, event | category | flops | bytes accessed | tf_op | source)
XLA Modules:
  0.0 1264.9 jit_solution(361143442329686264)
XLA Ops:
  28.3 9.4 all_gather.44
  56.2 11.6 all-gather.15.cloned.1.call-done
  72.0 22.0 %all-gather.13.cloned.1.call-done = bf16[6144,192]{0,1:T(8,128)(2,1)} async-done(((bf16[1536,192]{0,1:T(8,128)(2,1)}), bf16[6144,192]{0,1:T(8,128)(2,1)}) %all-gather.13.cloned.1.call-update) | async-done | bytes 2359312 | tf_op jit(solution)/shard_map/all_gather | solution.py:112
  99.5 67.6 %while.33 = (s32[]{:T(128)}, f32[3,1536,1]{1,0,2:T(4,128)S(1)}, f32[3,1536,1]{1,0,2:T(4,128)S(1)}, f32[3,1536,64]{1,2,0:T(8,128)}, s32[8]{0:T(128)}, /*index=5*/...) while((s32[]{:T(128)}, f32[3,1536,1]{1,0,2:T(4,128)S(1)}, ...), condition=%wide.region_10.11_spmd.clone, body=%wide.region_4.10_spmd.clone.sunk | while | flops 949046784 | bytes 107690344 | solution.py:165
  101.4 26.0 %conditional.6 = ((f32[3,1536,1]{1,0,2:T(4,128)S(1)}, f32[3,1536,1]{1,0,2:T(4,128)S(1)}, f32[3,1536,64]{1,2,0:T(8,128)})) conditional(s32[]{:T(128)} %convert_element_type.503, (f32[3,1536,1]{1,0,2:T(4,128)S(1)}, f32[3,1536,1]{1,0,2:T(4,128)S(1)}, f32[3,1536,64]{1,2,0:T(8,128)}) %tuple.94, (s32[1536]{0:T(1024)S(1)}, s32[]{:T(128)}, s32[2]{0:T(128)}, ...), branch_computations={%region_5.5_spmd, %region_6.9_spmd} | conditional | flops 949046784 | bytes 107683920 | solution.py:158
  119.2 8.2 fusion.5
  129.3 26.0 %conditional.6 = ((f32[3,1536,1]{1,0,2:T(4,128)S(1)}, f32[3,1536,1]{1,0,2:T(4,128)S(1)}, f32[3,1536,64]{1,2,0:T(8,128)})) conditional(s32[]{:T(128)} %convert_element_type.503, (f32[3,1536,1]{1,0,2:T(4,128)S(1)}, f32[3,1536,1]{1,0,2:T(4,128)S(1)}, f32[3,1536,64]{1,2,0:T(8,128)}) %tuple.94, (s32[1536]{0:T(1024)S(1)}, s32[]{:T(128)}, s32[2]{0:T(128)}, ...), branch_computations={%region_5.5_spmd, %region_6.9_spmd} | conditional | flops 949046784 | bytes 107683920 | solution.py:158
  147.1 8.2 fusion.5
  191.0 232.3 %all-reduce.16.cloned.1.call-done = bf16[1536,768]{1,0:T(8,128)(2,1)} async-done(((bf16[1536,768]{1,0:T(8,128)(2,1)}), bf16[1536,768]{1,0:T(8,128)(2,1)}) %all-reduce.16.cloned.1.call-update) | async-done | bytes 2359312 | tf_op jit(solution)/shard_map/psum | solution.py:173
  434.4 8.7 fusion.94
  448.7 94.1 %all-reduce.18.cloned.1.call-done = bf16[1536,768]{1,0:T(8,128)(2,1)} async-done(((bf16[1536,768]{1,0:T(8,128)(2,1)}), bf16[1536,768]{1,0:T(8,128)(2,1)}) %all-reduce.18.cloned.1.call-update) | async-done | bytes 2359312 | tf_op jit(solution)/shard_map/psum | solution.py:190
  559.0 84.0 %while.34 = (s32[]{:T(128)}, f32[1536,3,64]{0,2,1:T(8,128)S(1)}, bf16[8,768,3,64]{1,3,2,0:T(8,128)(2,1)}, bf16[8,768,3,64]{1,3,2,0:T(8,128)(2,1)}, s32[8]{0:T(12...) while((s32[]{:T(128)}, f32[1536,3,64]{0,2,1:T(8,128)S(1)}, ...), condition=%wide.region_22.23_spmd.clone, body=%wide.region_18.22_spmd.clone.sunk | while | flops 2304153600 | bytes 77088104 | solution.py:230
  560.9 30.3 %conditional.7 = (f32[1536,3,64]{0,2,1:T(8,128)S(1)}, bf16[1,768,3,64]{1,3,2,0:T(8,128)(2,1)S(1)}, bf16[1,768,3,64]{1,3,2,0:T(8,128)(2,1)S(1)}) conditional(s32[]{:T(128)} %convert_element_type.504, f32[1536,3,64]{0,2,1:T(8,128)S(1)} %get-tuple-element.886, (s32[1536]{0:T(1024)S(1)}, s32[]{:T(128)}, s32[2]{0:T(128)}, s32[]{:T(128)}, ...), branch_computations={%region_19.19_spmd, %region_20.21_spmd} | conditional | flops 2304153600 | bytes 75901512 | solution.py:228
  563.6 8.1 fusion.37
  594.1 30.4 %conditional.7 = (f32[1536,3,64]{0,2,1:T(8,128)S(1)}, bf16[1,768,3,64]{1,3,2,0:T(8,128)(2,1)S(1)}, bf16[1,768,3,64]{1,3,2,0:T(8,128)(2,1)S(1)}) conditional(s32[]{:T(128)} %convert_element_type.504, f32[1536,3,64]{0,2,1:T(8,128)S(1)} %get-tuple-element.886, (s32[1536]{0:T(1024)S(1)}, s32[]{:T(128)}, s32[2]{0:T(128)}, s32[]{:T(128)}, ...), branch_computations={%region_19.19_spmd, %region_20.21_spmd} | conditional | flops 2304153600 | bytes 75901512 | solution.py:228
  596.7 8.1 fusion.37
  667.2 194.4 %reduce-scatter.18.cloned.1.call-done = bf16[1536,192]{0,1:T(8,128)(2,1)} async-done(((bf16[6144,192]{0,1:T(8,128)(2,1)}), bf16[1536,192]{0,1:T(8,128)(2,1)}) %reduce-scatter.18.cloned.1.call-update) | async-done | bytes 589840 | tf_op jit(solution)/shard_map/reduce_scatter | solution.py:242
  864.1 33.1 %reduce-scatter.16.cloned.1.call-done = bf16[1536,192]{0,1:T(8,128)(2,1)} async-done(((bf16[6144,192]{0,1:T(8,128)(2,1)}), bf16[1536,192]{0,1:T(8,128)(2,1)}) %reduce-scatter.16.cloned.1.call-update) | async-done | bytes 589840 | tf_op jit(solution)/shard_map/reduce_scatter | solution.py:236
  939.0 20.2 %reduce-scatter.22.cloned.1.call-done = bf16[384,576]{1,0:T(8,128)(2,1)} async-done(((bf16[768,576]{1,0:T(8,128)(2,1)}), bf16[384,576]{1,0:T(8,128)(2,1)}) %reduce-scatter.22.cloned.1.call-update) | async-done | bytes 442384
  963.8 19.9 %reduce-scatter.20.cloned.1.call-done = bf16[384,768]{1,0:T(8,128)(2,1)} async-done(((bf16[768,768]{1,0:T(8,128)(2,1)}), bf16[384,768]{1,0:T(8,128)(2,1)}) %reduce-scatter.20.cloned.1.call-update) | async-done | bytes 589840 | tf_op jit(solution)/shard_map/reduce_scatter | solution.py:309
  996.7 48.7 %all-reduce.22.cloned.1.call-done = (bf16[3,384,192]{1,2,0:T(8,128)(2,1)}, bf16[192,384]{1,0:T(8,128)(2,1)}, bf16[384,768]{1,0:T(8,128)(2,1)}, bf16[768,384]{1,0:T(8,128)(2,1)}) async-done(((bf16[3,384,192]{1,2,0:T(8,128)(2,1)}, bf16[192,384]{1,0:T(8,128)(2,1)}, bf16[384,768]{1,0:T(8,128)(2,1)}, bf16[768,384]{1,0:T(8,128)(2,1)}), (bf16[3,384,192]{1,2,0:T(8,128)(2,1)}, bf16[192,384]{1,0:T(8,128)(2,1)}, ...) | async-done | bytes 1769488 | tf_op jit(solution)/shard_map/psum | solution.py:327
  1053.4 167.6 %all-reduce.20.cloned.1.call-done = (bf16[1536,768]{1,0:T(8,128)(2,1)}, bf16[1536,768]{1,0:T(8,128)(2,1)}) async-done(((bf16[1536,768]{1,0:T(8,128)(2,1)}, bf16[1536,768]{1,0:T(8,128)(2,1)}), (bf16[1536,768]{1,0:T(8,128)(2,1)}, bf16[1536,768]{1,0:T(8,128)(2,1)})) %all-reduce.20.cloned.1.call-update) | async-done | bytes 4718608 | tf_op jit(solution)/shard_map/psum | solution.py:180
  1229.1 8.1 all-reduce.10
  1248.1 9.5 add_add_fusion.2
  (385 shorter events, 324.6 us)
Async XLA Ops:
  8.0 59.8 %all-gather.15.cloned.1.call-start = ((), (), s32[]{:S(2)}) async-start(), calls=%async_computation.8 | async-start | bytes 2949120 | tf_op jit(solution)/shard_map/all_gather | solution.py:113
  42.1 51.9 %all-gather.13.cloned.1.call-start = ((), (), s32[]{:S(2)}) async-start(), calls=%async_computation.7 | async-start | bytes 2949120 | tf_op jit(solution)/shard_map/all_gather | solution.py:112
  45.6 377.8 %all-reduce.16.cloned.1.call-start = ((), (), s32[]{:S(2)}) async-start(), calls=%async_computation.9 | async-start | bytes 4718592 | tf_op jit(solution)/shard_map/psum | solution.py:173
  171.6 255.7 %all-gather.17.cloned.1.call-start = ((), (), s32[]{:S(2)}) async-start(), calls=%async_computation.10 | async-start | bytes 1769472 | tf_op jit(solution)/shard_map/all_gather | solution.py:89
  172.2 262.2 %all-gather.19.cloned.1.call-start = ((), (), s32[]{:S(2)}) async-start(), calls=%async_computation.11 | async-start | bytes 1769472 | tf_op jit(solution)/shard_map/all_gather | solution.py:91
  172.8 370.0 %all-reduce.18.cloned.1.call-start = ((), (), s32[]{:S(2)}) async-start(), calls=%async_computation.12 | async-start | bytes 4718592 | tf_op jit(solution)/shard_map/psum | solution.py:190
  177.2 374.1 %copy-start.34 = (f32[768]{0:T(1024)}, f32[768]{0:T(1024)S(1)}, u32[]{:S(2)}) copy-start(f32[768]{0:T(1024)S(1)} %reshape.282) | copy-start | bytes 9220
  181.6 245.7 %copy-start.46 = (f32[768]{0:T(1024)}, f32[768]{0:T(1024)S(1)}, u32[]{:S(2)}) copy-start(f32[768]{0:T(1024)S(1)} %reshape.283) | copy-start | bytes 9220
  186.0 365.3 %copy-start.24 = (f32[768]{0:T(1024)}, f32[768]{0:T(1024)S(1)}, u32[]{:S(2)}) copy-start(f32[768]{0:T(1024)S(1)} %reshape.281) | copy-start | bytes 9220
  191.0 243.4 %copy-start.48 = (f32[768]{0:T(1024)}, f32[768]{0:T(1024)S(1)}, u32[]{:S(2)}) copy-start(f32[768]{0:T(1024)S(1)} %reshape.284) | copy-start | bytes 9220
  448.0 413.6 %reduce-scatter.18.cloned.1.call-start = ((), (), s32[]{:S(2)}) async-start(), calls=%async_computation.14 | async-start | bytes 2949120 | tf_op jit(solution)/shard_map/reduce_scatter | solution.py:242
  648.1 249.1 %reduce-scatter.16.cloned.1.call-start = ((), (), s32[]{:S(2)}) async-start(), calls=%async_computation.13 | async-start | bytes 2949120 | tf_op jit(solution)/shard_map/reduce_scatter | solution.py:236
  653.2 277.8 %reduce-scatter.28.cloned.1.call-start = ((), (), s32[]{:S(2)}) async-start(), calls=%async_computation.19 | async-start | bytes 1769472
  660.6 276.7 %reduce-scatter.26.cloned.1.call-start = ((), (), s32[]{:S(2)}) async-start(), calls=%async_computation.18 | async-start | bytes 589824
  664.6 232.6 %copy-start.14 = (bf16[1536,768]{1,0:T(8,128)(2,1)S(1)}, bf16[1536,768]{1,0:T(8,128)(2,1)}, u32[]{:S(2)}) copy-start(bf16[1536,768]{1,0:T(8,128)(2,1)} %copy-done.13) | copy-start | bytes 7077892
  667.1 292.1 %reduce-scatter.22.cloned.1.call-start = ((), (), s32[]{:S(2)}) async-start(), calls=%async_computation.16 | async-start | bytes 1474560
  907.6 76.1 %reduce-scatter.20.cloned.1.call-start = ((), (), s32[]{:S(2)}) async-start(), calls=%async_computation.15 | async-start | bytes 1769472 | tf_op jit(solution)/shard_map/reduce_scatter | solution.py:309
  914.3 81.6 %reduce-scatter.24.cloned.1.call-start = ((), (), s32[]{:S(2)}) async-start(), calls=%async_computation.17 | async-start | bytes 73728
  927.0 118.5 %all-reduce.22.cloned.1.call-start = ((), (), s32[]{:S(2)}) async-start(), calls=%async_computation.21 | async-start | bytes 3538944 | tf_op jit(solution)/shard_map/psum | solution.py:327
  983.8 237.3 %all-reduce.20.cloned.1.call-start = ((), (), s32[]{:S(2)}) async-start(), calls=%async_computation.20 | async-start | bytes 9437184 | tf_op jit(solution)/shard_map/psum | solution.py:180
  989.5 233.6 %copy-start.21 = (f32[1536]{0:T(1024)S(1)}, f32[1536]{0:T(1024)}, u32[]{:S(2)}) copy-start(f32[1536]{0:T(1024)} %copy-done.20) | copy-start | bytes 18436
  989.5 233.6 %copy-start.37 = (f32[768]{0:T(1024)S(1)}, f32[768]{0:T(1024)}, u32[]{:S(2)}) copy-start(f32[768]{0:T(1024)} %copy-done.36) | copy-start | bytes 9220
  1051.3 175.0 %copy-start.39 = (f32[1536]{0:T(1024)S(1)}, f32[1536]{0:T(1024)}, u32[]{:S(2)}) copy-start(f32[1536]{0:T(1024)} %copy-done.38) | copy-start | bytes 18436
  1051.3 175.0 %copy-start.28 = (f32[1536]{0:T(1024)S(1)}, f32[1536]{0:T(1024)}, u32[]{:S(2)}) copy-start(f32[1536]{0:T(1024)} %copy-done.27) | copy-start | bytes 18436
  (53 other events, 735.3 us)
Sparse Core Ops, SparseCore 0:
  42.2 25.5 all-gather.14
  69.9 24.0 all-gather.12
  171.7 251.5 all-reduce.15
  448.1 94.6 all-reduce.17
  648.2 213.3 reduce-scatter.17
  864.1 33.0 reduce-scatter.15
  900.0 21.7 reduce-scatter.27
  924.1 13.1 reduce-scatter.25
  939.6 19.5 reduce-scatter.21
  961.9 21.7 reduce-scatter.19
  985.9 9.8 reduce-scatter.23
  998.9 46.5 all-reduce.21
  1048.6 172.3 all-reduce.19
Sparse Core Ops, SparseCore 1:
  173.6 178.5 all-gather.16
  353.6 22.6 all-gather.18
where the time goes:
time: 1270 us; the launch traced here: 1260 us
  waiting for transfers between devices  849 us (67%)
  matrix products  143 us (11%)
  other arithmetic  88.6 us (7%)
  local copies, waits for them, and re-layouts  88.5 us (7%)
  blocking collectives  65.8 us (5%)
  between operations  17.2 us (1%)
    psum x1, waiting for transfers between devices, on_device(): lax.psum(attn_partial.astype(jnp.bfloat16), 'tp').astype(jnp.float32)  232 us
    reduce_scatter x1, waiting for transfers between devices, on_device(): lax.psum_scatter(value_terms.reshape(block_count * block_rows, local_widt...  194 us
    psum x1, waiting for transfers between devices, on_device(): lax.psum(ff_partial.astype(jnp.bfloat16), 'tp').astype(jnp.float32)  168 us
    psum x1, waiting for transfers between devices, on_device(): lax.psum(norm_two_partial.astype(jnp.bfloat16), 'tp').astype(jnp.float32)  94.1 us
    psum x1, waiting for transfers between devices, on_device(): lax.psum(part_qkv.astype(jnp.bfloat16), 'ctx').astype(jnp.float32)  48.7 us
    unnamed x147, local copies, waits for them, and re-layouts  40.9 us
    reduce_scatter x1, waiting for transfers between devices, on_device(): lax.psum_scatter(key_terms.reshape(block_count * block_rows, local_width)...  33.1 us
    unnamed x19, waiting for transfers between devices  25.6 us
  transfers between devices with their start and end apart: 15, of which 11 were waited for; matrix products, arithmetic and copies ran while one was open for 8% of the time, Pallas kernels for 0%

commit v1 on v0

v1 whole, which is shorter than its diff:
```python
import jax
import jax.numpy as jnp
from jax import lax
from jax.experimental import pallas as pl
from jax.experimental.pallas import tpu as pltpu
from jax.sharding import PartitionSpec as P

HEAD = 64


norm_epsilon = 1e-05
masked_score = -1e30


def layer_norm(inputs_f, norm_gain, norm_shift):
    centred = inputs_f - jnp.mean(inputs_f, axis=-1, keepdims=True)
    spread = jnp.mean(centred * centred, axis=-1, keepdims=True)
    return centred * lax.rsqrt(spread + norm_epsilon) * norm_gain + norm_shift


def smooth_act(inputs_f):
    return jax.nn.gelu(inputs_f, approximate=True)


def mat_product(left_side, right_side):
    return jnp.dot(left_side, right_side, preferred_element_type=jnp.float32)


def left_product(left_side, right_side):
    return lax.dot_general(
        left_side, right_side, (((0,), (0,)), ((), ())), preferred_element_type=jnp.float32
    )


def right_product(left_side, right_side):
    return lax.dot_general(
        left_side, right_side, (((1,), (1,)), ((), ())), preferred_element_type=jnp.float32
    )


def column_sums(matrix):
    return jnp.sum(matrix.astype(jnp.float32), axis=0)


LANES = 128
Q_BLOCK = 256
K_BLOCK = 512
VMEM_BYTES = 60 * 1024 * 1024


def doc_start(place, bound_one, bound_two):
    return jnp.where(place >= bound_two, bound_two, jnp.where(place >= bound_one, bound_one, 0))


def widen(piece, tail):
    return jnp.concatenate([piece, tail], axis=1)


def lay_out_heads(kv_ref, key_s, value_s):
    heads, rows_all, _ = key_s.shape
    width = heads * HEAD
    lane = lax.broadcasted_iota(jnp.int32, (K_BLOCK, LANES - HEAD), 1)
    ones = jnp.where(lane < 3, 1.0, 0.0).astype(jnp.bfloat16)

    def step(block, carry):
        rows = pl.ds(pl.multiple_of(block * K_BLOCK, K_BLOCK), K_BLOCK)
        slab = kv_ref[rows, :]
        for h in range(heads):
            key_s[h, rows, :] = widen(slab[:, h * HEAD : (h + 1) * HEAD], ones)
            value_s[h, rows, :] = widen(slab[:, width + h * HEAD : width + (h + 1) * HEAD], ones)
        return carry

    lax.fori_loop(0, rows_all // K_BLOCK, step, 0)


def block_ranges(first, place_ref):
    bound_one, bound_two = place_ref[0], place_ref[1]
    last = first + Q_BLOCK - 1
    begin = doc_start(first, bound_one, bound_two) // K_BLOCK
    end = last // K_BLOCK + 1
    clear_from = (doc_start(last, bound_one, bound_two) + K_BLOCK - 1) // K_BLOCK
    clear_from = jnp.minimum(jnp.maximum(clear_from, begin), end)
    clear_to = jnp.minimum(jnp.maximum((first + 1) // K_BLOCK, clear_from), end)
    return begin, clear_from, clear_to, end


def three_loops(ranges, visit, carry):
    begin, clear_from, clear_to, end = ranges
    carry = lax.fori_loop(begin, clear_from, lambda i, c: visit(i, c, True), carry)
    carry = lax.fori_loop(clear_from, clear_to, lambda i, c: visit(i, c, False), carry)
    return lax.fori_loop(clear_to, end, lambda i, c: visit(i, c, True), carry)


def attend_kernel(place_ref, q_ref, kv_ref, out_ref, qa_ref, key_s, value_s, acc_s):
    heads = key_s.shape[0]
    lay_out_heads(kv_ref, key_s, value_s)
    half = q_ref.shape[0] // 2
    bound_one, bound_two = place_ref[0], place_ref[1]
    lane = lax.broadcasted_iota(jnp.int32, (Q_BLOCK, LANES), 1)
    zeros = jnp.zeros((Q_BLOCK, LANES - HEAD), jnp.float32)

    for part in range(2):

        def q_step(block, carry0, part=part):
            first = place_ref[2 + part] + block * Q_BLOCK
            rows = pl.ds(pl.multiple_of(part * half + block * Q_BLOCK, Q_BLOCK), Q_BLOCK)
            q_all = q_ref[rows, :].astype(jnp.float32) * (HEAD**-0.5)
            q_wide = [widen(q_all[:, h * HEAD : (h + 1) * HEAD], zeros) for h in range(heads)]
            q_low = [q.astype(jnp.bfloat16) for q in q_wide]
            acc_s[...] = jnp.zeros_like(acc_s)
            q_place = first + lax.broadcasted_iota(jnp.int32, (Q_BLOCK, 1), 0)
            q_start = doc_start(q_place, bound_one, bound_two)

            def visit(kb, maxima, masked):
                keys = pl.ds(pl.multiple_of(kb * K_BLOCK, K_BLOCK), K_BLOCK)
                if masked:
                    k_place = kb * K_BLOCK + lax.broadcasted_iota(
                        jnp.int32, (Q_BLOCK, K_BLOCK), 1
                    )
                    allowed = (k_place <= q_place) & (k_place >= q_start)
                new_maxima = []
                for h in range(heads):
                    scores = right_product(q_low[h], key_s[h, keys, :])
                    if masked:
                        scores = jnp.where(allowed, scores, masked_score)
                    new_max = jnp.maximum(maxima[h], jnp.max(scores, axis=1, keepdims=True))
                    prob = jnp.exp(scores - new_max).astype(jnp.bfloat16)
                    acc_s[h] = acc_s[h] * jnp.exp(maxima[h] - new_max) + mat_product(
                        prob, value_s[h, keys, :]
                    )
                    new_maxima.append(new_max)
                return tuple(new_maxima)

            start = tuple(jnp.full((Q_BLOCK, 1), masked_score, jnp.float32) for _ in range(heads))
            maxima = three_loops(block_ranges(first, place_ref), visit, start)
            outs = []
            for h in range(heads):
                total = acc_s[h]
                row_sum = total[:, HEAD : HEAD + 1]
                outs.append(total[:, :HEAD] / row_sum)
                minus = -(maxima[h] + jnp.log(row_sum))
                high = minus.astype(jnp.bfloat16).astype(jnp.float32)
                middle = (minus - high).astype(jnp.bfloat16).astype(jnp.float32)
                wide = jnp.where(lane == HEAD, high, q_wide[h])
                wide = jnp.where(lane == HEAD + 1, middle, wide)
                wide = jnp.where(lane == HEAD + 2, minus - high - middle, wide)
                qa_ref[h, rows, :] = wide.astype(jnp.bfloat16)
            out_ref[rows, :] = jnp.concatenate(outs, axis=1)
            return carry0

        lax.fori_loop(0, half // Q_BLOCK, q_step, 0)


def attend_back_kernel(
    place_ref, qa_ref, go_ref, out_ref, kv_ref, dq_ref, dkv_ref, key_s, value_s, dk_s, dv_s, dq_s
):
    heads, rows_all, _ = key_s.shape
    lay_out_heads(kv_ref, key_s, value_s)
    dk_s[...] = jnp.zeros_like(dk_s)
    dv_s[...] = jnp.zeros_like(dv_s)
    half = go_ref.shape[0] // 2
    bound_one, bound_two = place_ref[0], place_ref[1]
    lane = lax.broadcasted_iota(jnp.int32, (Q_BLOCK, LANES), 1)
    zeros = jnp.zeros((Q_BLOCK, LANES - HEAD), jnp.float32)

    for part in range(2):

        def q_step(block, carry0, part=part):
            first = place_ref[2 + part] + block * Q_BLOCK
            rows = pl.ds(pl.multiple_of(part * half + block * Q_BLOCK, Q_BLOCK), Q_BLOCK)
            go_all = go_ref[rows, :].astype(jnp.float32)
            weighted = go_all * out_ref[rows, :]
            go_low, q_low = [], []
            for h in range(heads):
                cols = slice(h * HEAD, (h + 1) * HEAD)
                minus = -jnp.sum(weighted[:, cols], axis=1, keepdims=True)
                high = minus.astype(jnp.bfloat16).astype(jnp.float32)
                wide = widen(go_all[:, cols], zeros)
                wide = jnp.where(lane == HEAD, high, wide)
                wide = jnp.where(lane == HEAD + 1, minus - high, wide)
                go_low.append(wide.astype(jnp.bfloat16))
                q_low.append(qa_ref[h, rows, :])
            dq_s[...] = jnp.zeros_like(dq_s)
            q_place = first + lax.broadcasted_iota(jnp.int32, (1, Q_BLOCK), 1)
            q_start = doc_start(q_place, bound_one, bound_two)

            def visit(kb, carry, masked):
                keys = pl.ds(pl.multiple_of(kb * K_BLOCK, K_BLOCK), K_BLOCK)
                if masked:
                    k_place = kb * K_BLOCK + lax.broadcasted_iota(
                        jnp.int32, (K_BLOCK, Q_BLOCK), 0
                    )
                    allowed = (k_place <= q_place) & (k_place >= q_start)
                for h in range(heads):
                    key_block = key_s[h, keys, :]
                    scores = right_product(key_block, q_low[h])
                    if masked:
                        scores = jnp.where(allowed, scores, masked_score)
                    prob = jnp.exp(scores)
                    grad_prob = right_product(value_s[h, keys, :], go_low[h])
                    grad_scores = (prob * grad_prob).astype(jnp.bfloat16)
                    dv_s[h, keys, :] += mat_product(prob.astype(jnp.bfloat16), go_low[h])
                    dk_s[h, keys, :] += mat_product(grad_scores, q_low[h])
                    dq_s[h] += left_product(grad_scores, key_block)
                return carry

            three_loops(block_ranges(first, place_ref), visit, 0)
            dq_ref[rows, :] = jnp.concatenate(
                [dq_s[h][:, :HEAD] * (HEAD**-0.5) for h in range(heads)], axis=1
            ).astype(jnp.bfloat16)
            return carry0

        lax.fori_loop(0, half // Q_BLOCK, q_step, 0)

    def store(block, carry):
        rows = pl.ds(pl.multiple_of(block * K_BLOCK, K_BLOCK), K_BLOCK)
        dkv_ref[rows, :] = jnp.concatenate(
            [dk_s[h, rows, :][:, :HEAD] for h in range(heads)]
            + [dv_s[h, rows, :][:, :HEAD] for h in range(heads)],
            axis=1,
        ).astype(jnp.bfloat16)
        return carry

    lax.fori_loop(0, rows_all // K_BLOCK, store, 0)


def in_vmem(count):
    return [pl.BlockSpec(memory_space=pltpu.VMEM)] * count


def attend(place, queries, kv_all):
    rows, width = queries.shape
    rows_all = kv_all.shape[0]
    heads = width // HEAD
    pairs = rows * rows_all * heads // 2
    return pl.pallas_call(
        attend_kernel,
        out_shape=(
            jax.ShapeDtypeStruct((rows, width), jnp.float32),
            jax.ShapeDtypeStruct((heads, rows, LANES), jnp.bfloat16),
        ),
        in_specs=[pl.BlockSpec(memory_space=pltpu.SMEM)] + in_vmem(2),
        out_specs=tuple(in_vmem(2)),
        scratch_shapes=[
            pltpu.VMEM((heads, rows_all, LANES), jnp.bfloat16),
            pltpu.VMEM((heads, rows_all, LANES), jnp.bfloat16),
            pltpu.VMEM((heads, Q_BLOCK, LANES), jnp.float32),
        ],
        compiler_params=pltpu.CompilerParams(vmem_limit_bytes=VMEM_BYTES),
        cost_estimate=pl.CostEstimate(
            flops=pairs * 4 * 4 * HEAD, bytes_accessed=8 << 20, transcendentals=pairs
        ),
    )(place, queries, kv_all)


def attend_back(place, queries_wide, grad_out, attn_out, kv_all):
    rows, width = grad_out.shape
    rows_all = kv_all.shape[0]
    heads = width // HEAD
    pairs = rows * rows_all * heads // 2
    return pl.pallas_call(
        attend_back_kernel,
        out_shape=(
            jax.ShapeDtypeStruct((rows, width), jnp.bfloat16),
            jax.ShapeDtypeStruct((rows_all, 2 * width), jnp.bfloat16),
        ),
        in_specs=[pl.BlockSpec(memory_space=pltpu.SMEM)] + in_vmem(4),
        out_specs=tuple(in_vmem(2)),
        scratch_shapes=[
            pltpu.VMEM((heads, rows_all, LANES), jnp.bfloat16),
            pltpu.VMEM((heads, rows_all, LANES), jnp.bfloat16),
            pltpu.VMEM((heads, rows_all, LANES), jnp.float32),
            pltpu.VMEM((heads, rows_all, LANES), jnp.float32),
            pltpu.VMEM((heads, Q_BLOCK, LANES), jnp.float32),
        ],
        compiler_params=pltpu.CompilerParams(vmem_limit_bytes=VMEM_BYTES),
        cost_estimate=pl.CostEstimate(
            flops=pairs * 10 * 4 * HEAD, bytes_accessed=12 << 20, transcendentals=pairs
        ),
    )(place, queries_wide, grad_out, attn_out, kv_all)


def swap_halves(rows):
    size = lax.axis_size("ctx")
    half = rows.shape[0] // 2
    moved = lax.ppermute(rows[half:], "ctx", [(i, size - 1 - i) for i in range(size)])
    return jnp.concatenate([rows[:half], moved], axis=0)


def partner(value, distance):
    size = lax.axis_size("ctx")
    return lax.ppermute(value, "ctx", [(i, i ^ distance) for i in range(size)])


def halve(block, distance):
    bit = (lax.axis_index("ctx") // distance) % 2
    split = block.reshape(block.shape[:-2] + (2, block.shape[-2] // 2, block.shape[-1]))
    axis = split.ndim - 3
    keep = lax.dynamic_index_in_dim(split, bit, axis, keepdims=False)
    send = lax.dynamic_index_in_dim(split, 1 - bit, axis, keepdims=False)
    got = partner(send, distance)
    return (keep.astype(jnp.float32) + got.astype(jnp.float32)).astype(jnp.bfloat16)


def unhalve(block, distance):
    bit = (lax.axis_index("ctx") // distance) % 2
    other = partner(block, distance)
    low = jnp.where(bit == 0, block, other)
    high = jnp.where(bit == 0, other, block)
    return jnp.concatenate([low, high], axis=-2)


def reduce_shards(block):
    size = lax.axis_size("ctx")
    distances = [1 << i for i in range(size.bit_length() - 1)]
    block = halve(block, 1)
    if block.shape[0] == 2:
        bit = lax.axis_index("fsdp")
        keep = lax.dynamic_index_in_dim(block, bit, 0, keepdims=False)
        send = lax.dynamic_index_in_dim(block, 1 - bit, 0, keepdims=False)
        got = lax.ppermute(send, "fsdp", [(0, 1), (1, 0)])
        block = (keep.astype(jnp.float32) + got.astype(jnp.float32)).astype(jnp.bfloat16)
    else:
        block = lax.psum_scatter(block, "fsdp", scatter_dimension=0, tiled=False)
    for distance in distances[1:]:
        block = halve(block, distance)
    for distance in distances[::-1]:
        block = unhalve(block, distance)
    return block


def on_device(
    tokens,
    cotangent,
    doc_lengths,
    ln1_gain,
    ln1_bias,
    ln2_gain,
    ln2_bias,
    w_qkv,
    qv_bias,
    w_out,
    out_bias,
    w_in,
    in_bias,
    w_back,
    back_bias,
):
    rows_here = tokens.shape[0]
    ctx_size = lax.axis_size("ctx")
    ctx_place = lax.axis_index("ctx")
    fsdp = lax.axis_size("fsdp")
    model = tokens.shape[1]
    part_d = model // fsdp
    qkv_full = lax.all_gather(w_qkv, "fsdp", axis=1, tiled=True)
    vectors = jnp.concatenate(
        [
            ln1_gain,
            ln1_bias,
            ln2_gain,
            ln2_bias,
            out_bias,
            back_bias,
            qv_bias[0],
            qv_bias[1],
            in_bias,
        ]
    )
    vectors = lax.all_gather(vectors, "fsdp", axis=0).astype(jnp.float32)
    sizes = [part_d] * 6 + [qv_bias.shape[1]] * 2 + [in_bias.shape[0]]
    pieces, offset = [], 0
    for size in sizes:
        pieces.append(vectors[:, offset : offset + size].reshape(fsdp * size))
        offset += size
    gain_one, shift_one, gain_two, shift_two, out_shift, back_shift, q_shift, v_shift, in_shift = (
        pieces
    )
    out_full = lax.all_gather(w_out, "fsdp", axis=1, tiled=True)
    in_full = lax.all_gather(w_in, "fsdp", axis=0, tiled=True)
    back_full = lax.all_gather(w_back, "fsdp", axis=1, tiled=True)
    local_width = qkv_full.shape[2]
    tokens_f = tokens.astype(jnp.float32)
    cot_f = cotangent.astype(jnp.float32)
    normed_one = layer_norm(tokens_f, gain_one, shift_one).astype(jnp.bfloat16)
    key_rows = mat_product(normed_one, qkv_full[1]).astype(jnp.bfloat16)
    value_rows = (mat_product(normed_one, qkv_full[2]) + v_shift).astype(jnp.bfloat16)
    kv_all = lax.all_gather(
        jnp.concatenate([key_rows, value_rows], axis=1), "ctx", axis=0, tiled=True
    )
    queries = (mat_product(normed_one, qkv_full[0]) + q_shift).astype(jnp.bfloat16)
    queries = swap_halves(queries)
    bounds = jnp.cumsum(doc_lengths[0])[:-1]
    half = rows_here // 2
    starts = jnp.stack([ctx_place * rows_here, (ctx_size - 1 - ctx_place) * rows_here + half])
    place = jnp.concatenate([bounds, starts]).astype(jnp.int32)
    attn_out, queries_wide = attend(place, queries, kv_all)
    attended = swap_halves(attn_out.astype(jnp.bfloat16))
    attn_partial = mat_product(attended, out_full)
    residual = (
        tokens_f + lax.psum(attn_partial.astype(jnp.bfloat16), "tp").astype(jnp.float32) + out_shift
    )
    normed_two = layer_norm(residual, gain_two, shift_two).astype(jnp.bfloat16)
    hidden = mat_product(normed_two, in_full) + in_shift
    active, gelu_pull = jax.vjp(smooth_act, hidden)
    active = active.astype(jnp.bfloat16)
    grad_active = right_product(cotangent, back_full)
    grad_hidden = gelu_pull(grad_active)[0].astype(jnp.bfloat16)
    norm_two_partial = right_product(grad_hidden, in_full)
    grad_normed_two = lax.psum(norm_two_partial.astype(jnp.bfloat16), "tp").astype(jnp.float32)
    ff_partial = mat_product(active, back_full)
    mixed = (
        residual + lax.psum(ff_partial.astype(jnp.bfloat16), "tp").astype(jnp.float32) + back_shift
    ).astype(jnp.bfloat16)
    back_shift_grad = column_sums(cotangent)
    back_grad = left_product(cotangent, active).astype(jnp.bfloat16)
    in_shift_grad = column_sums(grad_hidden)
    in_grad = left_product(normed_two, grad_hidden).astype(jnp.bfloat16)
    ff_width = in_grad.shape[1]
    ff_sum = reduce_shards(
        jnp.concatenate(
            [
                in_grad.reshape(fsdp, part_d, ff_width),
                back_grad.reshape(fsdp, part_d, ff_width),
            ],
            axis=1,
        )
    )
    unused, second_pull = jax.vjp(layer_norm, residual, gain_two, shift_two)
    grad_residual, gain_two_grad, shift_two_grad = second_pull(grad_normed_two)
    grad_residual = cot_f + grad_residual
    grad_attn = grad_residual.astype(jnp.bfloat16)
    out_shift_grad = column_sums(grad_attn)
    grad_attended = right_product(grad_attn, out_full).astype(jnp.bfloat16)
    out_grad = left_product(grad_attn, attended).astype(jnp.bfloat16)
    grad_swapped = swap_halves(grad_attended)
    grad_queries, kv_terms = attend_back(place, queries_wide, grad_swapped, attn_out, kv_all)
    grad_queries = swap_halves(grad_queries)
    grad_kv = lax.psum_scatter(kv_terms, "ctx", scatter_dimension=0, tiled=True)
    grad_keys = grad_kv[:, :local_width]
    grad_values = grad_kv[:, local_width:]
    norm_one_partial = (
        right_product(grad_queries, qkv_full[0])
        + right_product(grad_keys, qkv_full[1])
        + right_product(grad_values, qkv_full[2])
    )
    grad_normed_one = lax.psum(norm_one_partial.astype(jnp.bfloat16), "tp").astype(jnp.float32)
    unused, first_pull = jax.vjp(layer_norm, tokens_f, gain_one, shift_one)
    grad_tokens, gain_one_grad, shift_one_grad = first_pull(grad_normed_one)
    input_rows = grad_residual + grad_tokens
    head_parts = [
        part.astype(jnp.bfloat16).reshape(fsdp, part_d, local_width)
        for part in (
            left_product(normed_one, grad_queries),
            left_product(normed_one, grad_keys),
            left_product(normed_one, grad_values),
            out_grad,
        )
    ]
    head_sum = reduce_shards(jnp.concatenate(head_parts, axis=1))
    vector_parts = [
        part.reshape(fsdp, -1)
        for part in (
            gain_one_grad,
            shift_one_grad,
            gain_two_grad,
            shift_two_grad,
            out_shift_grad,
            back_shift_grad,
            column_sums(grad_queries),
            column_sums(grad_values),
            in_shift_grad,
        )
    ]
    vector_sum = jnp.concatenate(vector_parts, axis=1).reshape(-1)
    vector_sum = lax.psum(vector_sum, ("fsdp", "ctx")).reshape(fsdp, -1)
    vector_sum = lax.dynamic_index_in_dim(vector_sum, lax.axis_index("fsdp"), 0, keepdims=False)
    vector_out, offset = [], 0
    for size in sizes:
        vector_out.append(vector_sum[offset : offset + size])
        offset += size
    head_sum = head_sum.astype(jnp.float32)
    qkv_sum = head_sum[: 3 * part_d].reshape(3, part_d, local_width)
    out_sum = head_sum[3 * part_d :].T
    ff_sum = ff_sum.astype(jnp.float32)
    return (
        mixed,
        input_rows,
        vector_out[0],
        vector_out[1],
        vector_out[2],
        vector_out[3],
        qkv_sum,
        jnp.stack([vector_out[6], vector_out[7]]),
        out_sum,
        vector_out[4],
        ff_sum[:part_d],
        vector_out[8],
        ff_sum[part_d:].T,
        vector_out[5],
    )


def solution(mesh):
    return jax.shard_map(
        on_device,
        mesh=mesh,
        in_specs=(
            P(("fsdp", "ctx"), None),
            P(("fsdp", "ctx"), None),
            P("fsdp", None),
            P("fsdp"),
            P("fsdp"),
            P("fsdp"),
            P("fsdp"),
            P(None, "fsdp", "tp"),
            P(None, ("tp", "fsdp")),
            P("tp", "fsdp"),
            P("fsdp"),
            P("fsdp", "tp"),
            P(("tp", "fsdp")),
            P("tp", "fsdp"),
            P("fsdp"),
        ),
        out_specs=(
            P(("fsdp", "ctx"), None),
            P(("fsdp", "ctx"), None),
            P("fsdp"),
            P("fsdp"),
            P("fsdp"),
            P("fsdp"),
            P(None, "fsdp", "tp"),
            P(None, ("tp", "fsdp")),
            P("tp", "fsdp"),
            P("fsdp"),
            P("fsdp", "tp"),
            P(("tp", "fsdp")),
            P("tp", "fsdp"),
            P("fsdp"),
        ),
        check_vma=False,
    )
```

time: 1270 us -> 765 us (0.60)
  waiting for transfers between devices: 849 us -> 402 us
  matrix products: 143 us -> 57.9 us
  starting transfers between devices: 1.03 us -> 80 us
  local copies, waits for them, and re-layouts: 88.5 us -> 38.5 us
  Pallas kernels: 0 us -> 46.3 us
  other arithmetic: 88.6 us -> 67.2 us
  blocking collectives: 65.8 us -> 50.9 us
    reduce_scatter x3 -> x1, waiting for transfers between devices: 247 us -> 3.08 us  [on_device(): grad_kv = lax.psum_scatter(kv_terms, 'ctx', scatter_dimension=0, tiled=True)]
    psum x1, waiting for transfers between devices: 232 us -> 95.3 us  [on_device(): lax.psum(attn_partial.astype(jnp.bfloat16), 'tp').astype(jnp.float32)]
    ppermute x0 -> x14, starting transfers between devices: none -> 78.7 us  [the longest x8 40.9 us: partner(): return lax.ppermute(value, 'ctx', [(i, i ^ distance) for i in range(size)])]
    dot_general x14 -> x0, matrix products: 75.6 us -> none  [the longest x4 24.2 us: block_scores(): jnp.einsum('qhd,khd->hqk', query_heads, key_block, preferred_element_type...]
    ppermute x0 -> x14, waiting for transfers between devices: none -> 68.3 us  [the longest x4 40.1 us: swap_halves(): lax.ppermute(rows[half:], 'ctx', [(i, size - 1 - i) for i in range(size)])]
    psum x1, waiting for transfers between devices: 168 us -> 117 us  [on_device(): lax.psum(ff_partial.astype(jnp.bfloat16), 'tp').astype(jnp.float32)]
    psum x1 -> x0, waiting for transfers between devices: 48.7 us -> none  [on_device(): lax.psum(part_qkv.astype(jnp.bfloat16), 'ctx').astype(jnp.float32)]
    pallas_call x0 -> x2, Pallas kernels: none -> 46.3 us  [the longest x1 25.8 us: attend_back(): pl.pallas_call(attend_back_kernel, out_shape=(jax.ShapeDtypeStruct((rows,...]
  transfers between devices with their start and end apart: 15 -> 21, of which waited for: 11 -> 15; matrix products, arithmetic and copies ran while one was open for 8% -> 11% of each run, Pallas kernels for 0% -> 0%
where the time goes in v1:
time: 765 us; the launch traced here: 760 us
  waiting for transfers between devices  402 us (53%)
  starting transfers between devices  80 us (10%)
  other arithmetic  67.2 us (9%)
  matrix products  57.9 us (8%)
  blocking collectives  50.9 us (7%)
  Pallas kernels  46.3 us (6%)
  local copies, waits for them, and re-layouts  38.5 us (5%)
  between operations  16.9 us (2%)
    psum x1, waiting for transfers between devices, on_device(): lax.psum(ff_partial.astype(jnp.bfloat16), 'tp').astype(jnp.float32)  117 us
    psum x1, waiting for transfers between devices, on_device(): lax.psum(attn_partial.astype(jnp.bfloat16), 'tp').astype(jnp.float32)  95.3 us
    psum x1, waiting for transfers between devices, on_device(): lax.psum(norm_two_partial.astype(jnp.bfloat16), 'tp').astype(jnp.float32)  94.3 us
    ppermute x8, starting transfers between devices, partner(): return lax.ppermute(value, 'ctx', [(i, i ^ distance) for i in range(size)])  40.9 us
    ppermute x4, waiting for transfers between devices, swap_halves(): lax.ppermute(rows[half:], 'ctx', [(i, size - 1 - i) for i in range(size)])  40.1 us
    ppermute x4, starting transfers between devices, swap_halves(): lax.ppermute(rows[half:], 'ctx', [(i, size - 1 - i) for i in range(size)])  34.8 us
    pallas_call x1, Pallas kernels, attend_back(): pl.pallas_call(attend_back_kernel, out_shape=(jax.ShapeDtypeStruct((rows,...  25.8 us
    psum x1, blocking collectives, on_device(): vector_sum = lax.psum(vector_sum, ('fsdp', 'ctx')).reshape(fsdp, -1)  24 us
  transfers between devices with their start and end apart: 21, of which 15 were waited for; matrix products, arithmetic and copies ran while one was open for 11% of the time, Pallas kernels for 0%

profile of v1, /device:TPU:0, one launch (start us, length us, event | category | flops | bytes accessed | tf_op | source)
XLA Modules:
  0.0 759.9 jit_solution(4693961812155603826)
XLA Ops:
  10.8 4.9 concatenate.43
  16.0 9.6 %all-reduce = bf16[5760]{0:T(1024)(128)(2,1)S(1)} all-reduce(bf16[5760]{0:T(1024)(128)(2,1)S(1)} %dynamic-update-slice), channel_id=2, replica_groups=mesh['fsdp'=2,'ctx'=4,'tp'=4] {'fsdp'}, use_global_device_ids=true, to_apply=%add | all-reduce | flops 5760 | bytes 23040
  31.6 10.7 %all_gather.23 = bf16[3,768,192]{1,2,0:T(8,128)(2,1)S(1)} all-gather(bf16[3,384,192]{1,2,0:T(8,128)(2,1)} %param.22), channel_id=1, replica_groups=mesh['fsdp'=2,'ctx'=4,'tp'=4] {'fsdp'}, dimensions={1}, use_global_device_ids=true | all-gather | bytes 1327104 | tf_op jit(solution)/shard_map/all_gather | solution.py:355
  58.4 11.7 %collective-permute-done = bf16[768,192]{1,0:T(8,128)(2,1)S(1)} collective-permute-done((bf16[768,192]{1,0:T(8,128)(2,1)S(1)}, bf16[768,192]{1,0:T(8,128)(2,1)S(1)}, u32[]{:S(2)}, u32[]{:S(2)}) %collective-permute-start) | collective-permute-done | bytes 294944 | tf_op jit(solution)/shard_map/ppermute | solution.py:286
  71.1 23.0 %all-gather.5.cloned.1.call-done.kv_ref = bf16[6144,384]{1,0:T(8,128)(2,1)} async-done(((bf16[1536,384]{1,0:T(8,128)(2,1)}), bf16[6144,384]{1,0:T(8,128)(2,1)}) %all-gather.5.cloned.1.call-update) | async-done | bytes 4718608 | tf_op jit(solution)/shard_map/all_gather | solution.py:387
  94.2 20.5 %shard_map.254 = (f32[1536,192]{1,0:T(8,128)}, bf16[3,1536,128]{2,1,0:T(8,128)(2,1)}) custom-call(s32[4]{0:T(128)} %pad_add_fusion.place_ref, bf16[1536,192]{1,0:T(8,128)(2,1)} %pad_maximum_fusion.3.q_ref, bf16[6144,384]{1,0:T(8,128)(2,1)} %all-gather.5.cloned.1.call-done.kv_ref), custom_call_target="tpu_custom_call" | custom-call | flops 14495514624 | bytes 8388608 | tf_op jit(solution)/shard_map/pallas_call | solution.py:236
  116.2 33.2 %collective-permute-start.1 = (bf16[768,192]{1,0:T(8,128)(2,1)S(1)}, bf16[768,192]{1,0:T(8,128)(2,1)S(1)}, u32[]{:S(2)}, u32[]{:S(2)}) collective-permute-start(bf16[768,192]{1,0:T(8,128)(2,1)S(1)} %get-tuple-element.113), channel_id=1, source_target_pairs={{0,12},{4,8},{8,4},{12,0},{1,13},{5,9},{9,5},{13,1},{2,14},{6,10},... | collective-permute-start | bytes 884744 | tf_op jit(solution)/shard_map/ppermute | solution.py:286
  149.4 6.7 all_gather.25
  162.2 95.3 %all-reduce.6.cloned.1.call-done = bf16[1536,768]{1,0:T(8,128)(2,1)} async-done(((bf16[1536,768]{1,0:T(8,128)(2,1)}), bf16[1536,768]{1,0:T(8,128)(2,1)}) %all-reduce.6.cloned.1.call-update) | async-done | bytes 2359312 | tf_op jit(solution)/shard_map/psum | solution.py:400
  261.6 7.0 fusion.48
  268.5 8.7 %convert_reduce_fusion.4 = (f32[768]{0:T(1024)}, bf16[1536,768]{1,0:T(8,128)(2,1)S(1)}) fusion(f32[1536,768]{1,0:T(8,128)} %fusion.48, f32[768]{0:T(1024)S(1)} %add.219, bf16[1536,768]{1,0:T(8,128)(2,1)} %param.16, bf16[768,768]{1,0:T(8,128)(2,1)} %all-gather.9.cloned.1.call-done), kind=kOutput, calls=%fused_computation.38 | convolution fusion | flops 1839070464 | bytes 10622976 | tf_op jit(solution)/shard_map/dot_general | solution.py:36
  282.7 94.3 %all-reduce.8.cloned.1.call-done = bf16[1536,768]{1,0:T(8,128)(2,1)} async-done(((bf16[1536,768]{1,0:T(8,128)(2,1)}), bf16[1536,768]{1,0:T(8,128)(2,1)}) %all-reduce.8.cloned.1.call-update) | async-done | bytes 2359312 | tf_op jit(solution)/shard_map/psum | solution.py:409
  377.0 5.2 convert_reduce_fusion.1
  391.5 10.5 %collective-permute-done.2 = bf16[768,192]{1,0:T(8,128)(2,1)S(1)} collective-permute-done((bf16[768,192]{1,0:T(8,128)(2,1)S(1)}, bf16[768,192]{1,0:T(8,128)(2,1)S(1)}, u32[]{:S(2)}, u32[]{:S(2)}) %collective-permute-start.2) | collective-permute-done | bytes 294944 | tf_op jit(solution)/shard_map/ppermute | solution.py:286
  403.0 25.8 %shard_map.255 = (bf16[1536,192]{1,0:T(8,128)(2,1)}, bf16[6144,384]{1,0:T(8,128)(2,1)}) custom-call(s32[4]{0:T(128)} %pad_add_fusion.place_ref, bf16[3,1536,128]{2,1,0:T(8,128)(2,1)} %get-tuple-element.19.qa_ref, bf16[1536,192]{1,0:T(8,128)(2,1)} %pad_maximum_fusion.5.go_ref, f32[1536,192]{1,0:T(8,128)} %get-tuple-element.18.out_ref, ...), custom_call_target="tpu_custom_call" | custom-call | flops 36238786560 | bytes 12582912 | tf_op jit(solution)/shard_map/pallas_call | solution.py:261
  429.1 5.8 convolution_convert_fusion.5
  440.3 38.4 %collective-permute-start.9 = (bf16[2,384,768]{2,1,0:T(8,128)(2,1)}, bf16[2,384,768]{2,1,0:T(8,128)(2,1)}, u32[]{:S(2)}, u32[]{:S(2)}) collective-permute-start(bf16[2,384,768]{2,1,0:T(8,128)(2,1)} %dynamic-slice_bitcast_fusion), channel_id=1, source_target_pairs={{0,4},{4,0},{8,12},{12,8},{1,5},{5,1},{9,13},{13,9},{2,6},{6,2},{1... | collective-permute-start | bytes 3538952 | tf_op jit(solution)/shard_map/ppermute | solution.py:292
  485.1 7.2 convolution_convert_fusion.1
  492.3 6.9 collective-permute-done.10
  503.8 15.5 %collective-permute-done.3 = bf16[768,192]{1,0:T(8,128)(2,1)S(1)} collective-permute-done((bf16[768,192]{1,0:T(8,128)(2,1)S(1)}, bf16[768,192]{1,0:T(8,128)(2,1)S(1)}, u32[]{:S(2)}, u32[]{:S(2)}) %collective-permute-start.3) | collective-permute-done | bytes 294944 | tf_op jit(solution)/shard_map/ppermute | solution.py:286
  547.2 9.4 %collective-permute-done.12 = bf16[192,768]{1,0:T(8,128)(2,1)S(1)} collective-permute-done((bf16[192,768]{1,0:T(8,128)(2,1)S(1)}, bf16[192,768]{1,0:T(8,128)(2,1)S(1)}, u32[]{:S(2)}, u32[]{:S(2)}) %collective-permute-start.12) | collective-permute-done | bytes 294944 | tf_op jit(solution)/shard_map/ppermute | solution.py:292
  592.1 116.8 %all-reduce.10.cloned.1.call-done = (bf16[1536,768]{1,0:T(8,128)(2,1)}, bf16[1536,768]{1,0:T(8,128)(2,1)}) async-done(((bf16[1536,768]{1,0:T(8,128)(2,1)}, bf16[1536,768]{1,0:T(8,128)(2,1)}), (bf16[1536,768]{1,0:T(8,128)(2,1)}, bf16[1536,768]{1,0:T(8,128)(2,1)})) %all-reduce.10.cloned.1.call-update) | async-done | bytes 4718608 | tf_op jit(solution)/shard_map/psum | solution.py:412
  716.5 10.6 %add_add_fusion.2 = (f32[1536,768]{1,0:T(8,128)}, bf16[1536,768]{1,0:T(8,128)(2,1)}, f32[768]{0:T(1024)S(1)}) fusion(bf16[1536,768]{1,0:T(8,128)(2,1)S(1)} %copy-done, bf16[1536,768]{1,0:T(8,128)(2,1)} %get-tuple-element.94, bf16[1536,768]{1,0:T(8,128)(2,1)} %param.16, f32[1536]{0:T(1024)S(1)} %negate_multiply_fusion, f32[1536]{0:T(1024)S(1)} %multiply_multiply_fusion.2, ...), kind=kLoop, calls=%fused_computation.40 | loop fusion | flops 33029376 | bytes 21298176 | tf_op jit(solution)/shard_map/add | solution.py:449
  727.2 24.0 %psum.39 = f32[2,2880]{1,0:T(2,128)S(1)} all-reduce(f32[2,2880]{1,0:T(2,128)S(1)} %concatenate.49), channel_id=1, replica_groups=mesh['fsdp'=2,'ctx'=4,'tp'=4] {'fsdp','ctx'}, use_global_device_ids=true, to_apply=%region_23.24 | all-reduce | flops 5760 | bytes 46080 | tf_op jit(solution)/shard_map/psum | solution.py:475
  (247 shorter events, 141.3 us)
Async XLA Ops:
  8.0 86.1 %all-gather.5.cloned.1.call-start = ((), (), s32[]{:S(2)}) async-start(), calls=%async_computation.1 | async-start | bytes 5898240 | tf_op jit(solution)/shard_map/all_gather | solution.py:387
  52.9 204.6 %all-reduce.6.cloned.1.call-start = ((), (), s32[]{:S(2)}) async-start(), calls=%async_computation.2 | async-start | bytes 4718592 | tf_op jit(solution)/shard_map/psum | solution.py:400
  55.8 14.4 %collective-permute-start = (bf16[768,192]{1,0:T(8,128)(2,1)S(1)}, bf16[768,192]{1,0:T(8,128)(2,1)S(1)}, u32[]{:S(2)}, u32[]{:S(2)}) collective-permute-start(bf16[768,192]{1,0:T(8,128)(2,1)S(1)} %get-tuple-element.115), channel_id=1, source_target_pairs={{0,12},{4,8},{8,4},{12,0},{1,13},{5,9},{9,5},{13,1},{2,14},{6,10},... | collective-permute-start | bytes 884744 | tf_op jit(solution)/shard_map/ppermute | solution.py:286
  116.2 42.3 %collective-permute-start.1 = (bf16[768,192]{1,0:T(8,128)(2,1)S(1)}, bf16[768,192]{1,0:T(8,128)(2,1)S(1)}, u32[]{:S(2)}, u32[]{:S(2)}) collective-permute-start(bf16[768,192]{1,0:T(8,128)(2,1)S(1)} %get-tuple-element.113), channel_id=1, source_target_pairs={{0,12},{4,8},{8,4},{12,0},{1,13},{5,9},{9,5},{13,1},{2,14},{6,10},... | collective-permute-start | bytes 884744 | tf_op jit(solution)/shard_map/ppermute | solution.py:286
  160.7 100.8 %all-gather.7.cloned.1.call-start = ((), (), s32[]{:S(2)}) async-start(), calls=%async_computation.3 | async-start | bytes 1769472 | tf_op jit(solution)/shard_map/all_gather | solution.py:379
  161.3 107.2 %all-gather.9.cloned.1.call-start = ((), (), s32[]{:S(2)}) async-start(), calls=%async_computation.4 | async-start | bytes 1769472 | tf_op jit(solution)/shard_map/all_gather | solution.py:380
  161.9 215.1 %all-reduce.8.cloned.1.call-start = ((), (), s32[]{:S(2)}) async-start(), calls=%async_computation.5 | async-start | bytes 4718592 | tf_op jit(solution)/shard_map/psum | solution.py:409
  261.5 173.4 %copy-start.31 = (f32[1536]{0:T(1024)}, f32[1536]{0:T(1024)S(1)}, u32[]{:S(2)}) copy-start(f32[1536]{0:T(1024)S(1)} %fusion.42) | copy-start | bytes 18436
  282.2 242.3 %reduce-scatter.2.cloned.1.call-start = ((), (), s32[]{:S(2)}) async-start(), calls=%async_computation.6 | async-start | bytes 5898240 | tf_op jit(solution)/shard_map/reduce_scatter | solution.py:438
  390.5 11.4 %collective-permute-start.2 = (bf16[768,192]{1,0:T(8,128)(2,1)S(1)}, bf16[768,192]{1,0:T(8,128)(2,1)S(1)}, u32[]{:S(2)}, u32[]{:S(2)}) collective-permute-start(bf16[768,192]{1,0:T(8,128)(2,1)S(1)} %get-tuple-element.111), channel_id=1, source_target_pairs={{0,12},{4,8},{8,4},{12,0},{1,13},{5,9},{9,5},{13,1},{2,14},{6,10},... | collective-permute-start | bytes 884744 | tf_op jit(solution)/shard_map/ppermute | solution.py:286
  428.8 280.1 %all-reduce.10.cloned.1.call-start = ((), (), s32[]{:S(2)}) async-start(), calls=%async_computation.7 | async-start | bytes 9437184 | tf_op jit(solution)/shard_map/psum | solution.py:412
  440.3 41.2 %collective-permute-start.9 = (bf16[2,384,768]{2,1,0:T(8,128)(2,1)}, bf16[2,384,768]{2,1,0:T(8,128)(2,1)}, u32[]{:S(2)}, u32[]{:S(2)}) collective-permute-start(bf16[2,384,768]{2,1,0:T(8,128)(2,1)} %dynamic-slice_bitcast_fusion), channel_id=1, source_target_pairs={{0,4},{4,0},{8,12},{12,8},{1,5},{5,1},{9,13},{13,9},{2,6},{6,2},{1... | collective-permute-start | bytes 3538952 | tf_op jit(solution)/shard_map/ppermute | solution.py:292
  483.5 15.7 %collective-permute-start.10 = (bf16[384,768]{1,0:T(8,128)(2,1)S(1)}, bf16[384,768]{1,0:T(8,128)(2,1)S(1)}, u32[]{:S(2)}, u32[]{:S(2)}) collective-permute-start(bf16[384,768]{1,0:T(8,128)(2,1)S(1)} %dynamic-slice_bitcast_fusion.1), channel_id=1, source_target_pairs={{0,16},{16,0},{1,17},{17,1},{2,18},{18,2},{3,19},{19,3},{4,20},{20... | collective-permute-start | bytes 1769480 | tf_op jit(solution)/shard_map/ppermute | solution.py:321
  499.4 19.9 %collective-permute-start.3 = (bf16[768,192]{1,0:T(8,128)(2,1)S(1)}, bf16[768,192]{1,0:T(8,128)(2,1)S(1)}, u32[]{:S(2)}, u32[]{:S(2)}) collective-permute-start(bf16[768,192]{1,0:T(8,128)(2,1)S(1)} %get-tuple-element.109), channel_id=1, source_target_pairs={{0,12},{4,8},{8,4},{12,0},{1,13},{5,9},{9,5},{13,1},{2,14},{6,10},... | collective-permute-start | bytes 884744 | tf_op jit(solution)/shard_map/ppermute | solution.py:286
  500.9 45.2 %collective-permute-start.11 = (bf16[192,768]{1,0:T(8,128)(2,1)}, bf16[192,768]{1,0:T(8,128)(2,1)}, u32[]{:S(2)}, u32[]{:S(2)}) collective-permute-start(bf16[192,768]{1,0:T(8,128)(2,1)} %dynamic-slice_bitcast_fusion.2), channel_id=1, source_target_pairs={{0,8},{4,12},{8,0},{12,4},{1,9},{5,13},{9,1},{13,5},{2,10},{6,14},... | collective-permute-start | bytes 884744 | tf_op jit(solution)/shard_map/ppermute | solution.py:292
  546.0 10.6 %collective-permute-start.4 = (bf16[2,768,192]{1,2,0:T(8,128)(2,1)}, bf16[2,768,192]{1,2,0:T(8,128)(2,1)}, u32[]{:S(2)}, u32[]{:S(2)}) collective-permute-start(bf16[2,768,192]{1,2,0:T(8,128)(2,1)} %bitcast.102), channel_id=1, source_target_pairs={{0,4},{4,0},{8,12},{12,8},{1,5},{5,1},{9,13},{13,9},{2,6},{6,2},{1... | collective-permute-start | bytes 1769480 | tf_op jit(solution)/shard_map/ppermute | solution.py:292
  547.1 9.5 %collective-permute-start.12 = (bf16[192,768]{1,0:T(8,128)(2,1)S(1)}, bf16[192,768]{1,0:T(8,128)(2,1)S(1)}, u32[]{:S(2)}, u32[]{:S(2)}) collective-permute-start(bf16[192,768]{1,0:T(8,128)(2,1)S(1)} %fusion.38), channel_id=1, source_target_pairs={{0,8},{4,12},{8,0},{12,4},{1,9},{5,13},{9,1},{13,5},{2,10},{6,14},... | collective-permute-start | bytes 884744 | tf_op jit(solution)/shard_map/ppermute | solution.py:292
  558.9 9.1 %collective-permute-start.5 = (bf16[768,192]{0,1:T(8,128)(2,1)}, bf16[768,192]{0,1:T(8,128)(2,1)}, u32[]{:S(2)}, u32[]{:S(2)}) collective-permute-start(bf16[768,192]{0,1:T(8,128)(2,1)} %dynamic-slice_bitcast_fusion.3), channel_id=1, source_target_pairs={{0,16},{16,0},{1,17},{17,1},{2,18},{18,2},{3,19},{19,3},{4,20},{20... | collective-permute-start | bytes 884744 | tf_op jit(solution)/shard_map/ppermute | solution.py:321
  561.2 10.7 %collective-permute-start.13 = (bf16[384,768]{1,0:T(8,128)(2,1)}, bf16[384,768]{1,0:T(8,128)(2,1)}, u32[]{:S(2)}, u32[]{:S(2)}) collective-permute-start(bf16[384,768]{1,0:T(8,128)(2,1)} %pad_maximum_fusion.7), channel_id=1, source_target_pairs={{0,4},{4,0},{8,12},{12,8},{1,5},{5,1},{9,13},{13,9},{2,6},{6,2},{1... | collective-permute-start | bytes 1769480 | tf_op jit(solution)/shard_map/ppermute | solution.py:292
  571.3 5.9 collective-permute-start.6
  577.3 5.2 collective-permute-start.7
  583.4 5.6 collective-permute-start.8
  585.9 123.0 %copy-start.27 = (f32[1536]{0:T(1024)S(1)}, f32[1536]{0:T(1024)}, u32[]{:S(2)}) copy-start(f32[1536]{0:T(1024)} %copy-done.26) | copy-start | bytes 18436
  585.9 123.0 %copy-start.36 = (f32[768]{0:T(1024)S(1)}, f32[768]{0:T(1024)}, u32[]{:S(2)}) copy-start(f32[768]{0:T(1024)} %copy-done.35) | copy-start | bytes 9220
  (48 other events, 702.7 us)
Sparse Core Ops, SparseCore 0:
  53.1 41.0 all-gather.4
  160.8 96.6 all-reduce.5
  282.3 94.6 all-reduce.7
  428.9 95.5 reduce-scatter.1
  534.6 174.2 all-reduce.9
Sparse Core Ops, SparseCore 1:
  162.7 23.7 all-gather.6
  187.8 22.6 all-gather.8

commit v2 on v1

--- a/solution.py
+++ b/solution.py
@@ -228,6 +228,117 @@
     return [pl.BlockSpec(memory_space=pltpu.VMEM)] * count
 
 
+LINE_STEPS = 12
+
+
+def line_sum_kernel(x_ref, out_ref, land, cross, part, send_e, recv_e, send_c, recv_c):
+    me = lax.axis_index("tp")
+    edge_peer = me + 1 - 2 * (me % 2)
+    cross_peer = 3 - me
+    inner = (me == 1) | (me == 2)
+    step = x_ref.shape[0] // LINE_STEPS
+    barrier = pltpu.get_barrier_semaphore()
+    mesh_id = pl.DeviceIdType.MESH
+    pl.semaphore_signal(barrier, inc=1, device_id={"tp": edge_peer}, device_id_type=mesh_id)
+
+    @pl.when(inner)
+    def _():
+        pl.semaphore_signal(barrier, inc=1, device_id={"tp": cross_peer}, device_id_type=mesh_id)
+        pl.semaphore_wait(barrier, 2)
+
+    @pl.when(jnp.logical_not(inner))
+    def _():
+        pl.semaphore_wait(barrier, 1)
+
+    def rows_of(c):
+        return pl.ds(pl.multiple_of(c * step, step), step)
+
+    def edge_copy(c, source):
+        return pltpu.make_async_remote_copy(
+            src_ref=source.at[rows_of(c)],
+            dst_ref=land.at[rows_of(c)],
+            send_sem=send_e.at[c],
+            recv_sem=recv_e.at[c],
+            device_id={"tp": edge_peer},
+            device_id_type=mesh_id,
+        )
+
+    def cross_copy(c):
+        return pltpu.make_async_remote_copy(
+            src_ref=part.at[rows_of(c)],
+            dst_ref=cross.at[rows_of(c)],
+            send_sem=send_c.at[c],
+            recv_sem=recv_c.at[c],
+            device_id={"tp": cross_peer},
+            device_id_type=mesh_id,
+        )
+
+    def add(left, right, c):
+        total = left[rows_of(c), :].astype(jnp.float32) + right[rows_of(c), :].astype(jnp.float32)
+        return total.astype(jnp.bfloat16)
+
+    @pl.when(jnp.logical_not(inner))
+    def _():
+        @pl.loop(0, LINE_STEPS)
+        def _(c):
+            edge_copy(c, x_ref).start()
+
+        @pl.loop(0, LINE_STEPS)
+        def _(c):
+            edge_copy(c, x_ref).wait_recv()
+            out_ref[rows_of(c), :] = land[rows_of(c), :]
+
+        @pl.loop(0, LINE_STEPS)
+        def _(c):
+            edge_copy(c, x_ref).wait_send()
+
+    @pl.when(inner)
+    def _():
+        def first_half(c):
+            edge_copy(c, out_ref).wait_recv()
+            part[rows_of(c), :] = add(x_ref, land, c)
+            cross_copy(c).start()
+
+        def second_half(c):
+            cross_copy(c).wait_recv()
+            out_ref[rows_of(c), :] = add(part, cross, c)
+            edge_copy(c, out_ref).start()
+
+        first_half(0)
+
+        @pl.loop(1, LINE_STEPS)
+        def _(c):
+            first_half(c)
+            second_half(c - 1)
+
+        second_half(LINE_STEPS - 1)
+
+        @pl.loop(0, LINE_STEPS)
+        def _(c):
+            cross_copy(c).wait_send()
+            edge_copy(c, out_ref).wait_send()
+
+
+def line_sum(value, call):
+    if lax.axis_size("tp") != 4 or value.shape[0] % (16 * LINE_STEPS) != 0:
+        return lax.psum(value, "tp")
+    buffer = pltpu.VMEM(value.shape, value.dtype)
+    sems = pltpu.SemaphoreType.DMA((LINE_STEPS,))
+    return pl.pallas_call(
+        line_sum_kernel,
+        out_shape=jax.ShapeDtypeStruct(value.shape, value.dtype),
+        in_specs=in_vmem(1),
+        out_specs=in_vmem(1)[0],
+        scratch_shapes=[buffer, buffer, buffer, sems, sems, sems, sems],
+        compiler_params=pltpu.CompilerParams(
+            vmem_limit_bytes=VMEM_BYTES // 2, collective_id=call, has_side_effects=True
+        ),
+        cost_estimate=pl.CostEstimate(
+            flops=50_000_000_000, bytes_accessed=4 << 20, transcendentals=0
+        ),
+    )(value)
+
+
 def attend(place, queries, kv_all):
     rows, width = queries.shape
     rows_all = kv_all.shape[0]
@@ -308,6 +419,15 @@
     low = jnp.where(bit == 0, block, other)
     high = jnp.where(bit == 0, other, block)
     return jnp.concatenate([low, high], axis=-2)
+
+
+def sum_shards(vector):
+    size = lax.axis_size("ctx")
+    for i in range(size.bit_length() - 1):
+        vector = vector + partner(vector, 1 << i)
+    if lax.axis_size("fsdp") == 2:
+        return vector + lax.ppermute(vector, "fsdp", [(0, 1), (1, 0)])
+    return lax.psum(vector, "fsdp")
 
 
 def reduce_shards(block):
@@ -397,7 +517,7 @@
     attended = swap_halves(attn_out.astype(jnp.bfloat16))
     attn_partial = mat_product(attended, out_full)
     residual = (
-        tokens_f + lax.psum(attn_partial.astype(jnp.bfloat16), "tp").astype(jnp.float32) + out_shift
+        tokens_f + line_sum(attn_partial.astype(jnp.bfloat16), 0).astype(jnp.float32) + out_shift
     )
     normed_two = layer_norm(residual, gain_two, shift_two).astype(jnp.bfloat16)
     hidden = mat_product(normed_two, in_full) + in_shift
@@ -406,7 +526,7 @@
     grad_active = right_product(cotangent, back_full)
     grad_hidden = gelu_pull(grad_active)[0].astype(jnp.bfloat16)
     norm_two_partial = right_product(grad_hidden, in_full)
-    grad_normed_two = lax.psum(norm_two_partial.astype(jnp.bfloat16), "tp").astype(jnp.float32)
+    grad_normed_two = line_sum(norm_two_partial.astype(jnp.bfloat16), 1).astype(jnp.float32)
     ff_partial = mat_product(active, back_full)
     mixed = (
         residual + lax.psum(ff_partial.astype(jnp.bfloat16), "tp").astype(jnp.float32) + back_shift
@@ -443,7 +563,7 @@
         + right_product(grad_keys, qkv_full[1])
         + right_product(grad_values, qkv_full[2])
     )
-    grad_normed_one = lax.psum(norm_one_partial.astype(jnp.bfloat16), "tp").astype(jnp.float32)
+    grad_normed_one = line_sum(norm_one_partial.astype(jnp.bfloat16), 2).astype(jnp.float32)
     unused, first_pull = jax.vjp(layer_norm, tokens_f, gain_one, shift_one)
     grad_tokens, gain_one_grad, shift_one_grad = first_pull(grad_normed_one)
     input_rows = grad_residual + grad_tokens
@@ -472,7 +592,7 @@
         )
     ]
     vector_sum = jnp.concatenate(vector_parts, axis=1).reshape(-1)
-    vector_sum = lax.psum(vector_sum, ("fsdp", "ctx")).reshape(fsdp, -1)
+    vector_sum = sum_shards(vector_sum).reshape(fsdp, -1)
     vector_sum = lax.dynamic_index_in_dim(vector_sum, lax.axis_index("fsdp"), 0, keepdims=False)
     vector_out, offset = [], 0
     for size in sizes:

time: 765 us -> 659 us (0.86)
  waiting for transfers between devices: 402 us -> 77.7 us
  Pallas kernels: 46.3 us -> 365 us
  starting transfers between devices: 80 us -> 16.2 us
  blocking collectives: 50.9 us -> 29.4 us
    pallas_call x0 -> x3, Pallas kernels: none -> 254 us  [line_sum(): pl.pallas_call(line_sum_kernel, out_shape=jax.ShapeDtypeStruct(value.shap...]
    psum x2 -> x0, waiting for transfers between devices: 190 us -> none  [the longest x1 95.3 us: on_device(): lax.psum(attn_partial.astype(jnp.bfloat16), 'tp').astype(jnp.float32)]
    psum x1, waiting for transfers between devices: 117 us -> 0.01 us  [on_device(): lax.psum(ff_partial.astype(jnp.bfloat16), 'tp').astype(jnp.float32)]
    pallas_call x1, Pallas kernels: 25.8 us -> 60.6 us  [attend_back(): pl.pallas_call(attend_back_kernel, out_shape=(jax.ShapeDtypeStruct((rows,...]
    ppermute x4, starting transfers between devices: 34.8 us -> 0.22 us  [swap_halves(): lax.ppermute(rows[half:], 'ctx', [(i, size - 1 - i) for i in range(size)])]
    ppermute x8 -> x10, starting transfers between devices: 40.9 us -> 8.93 us  [partner(): return lax.ppermute(value, 'ctx', [(i, i ^ distance) for i in range(size)])]
    pallas_call x1, Pallas kernels: 20.5 us -> 50.2 us  [attend(): pl.pallas_call(attend_kernel, out_shape=(jax.ShapeDtypeStruct((rows, widt...]
    psum x1 -> x0, blocking collectives: 24 us -> none  [on_device(): vector_sum = lax.psum(vector_sum, ('fsdp', 'ctx')).reshape(fsdp, -1)]
  transfers between devices with their start and end apart: 21 -> 22, of which waited for: 15 -> 10; matrix products, arithmetic and copies ran while one was open for 11% -> 15% of each run, Pallas kernels for 0% -> 37%
where the time goes in v2:
time: 659 us; the launch traced here: 654 us
  Pallas kernels  365 us (55%)
  waiting for transfers between devices  77.7 us (12%)
  other arithmetic  60.4 us (9%)
  matrix products  53.9 us (8%)
  local copies, waits for them, and re-layouts  35.5 us (5%)
  blocking collectives  29.4 us (4%)
  starting transfers between devices  16.2 us (2%)
  between operations  15.7 us (2%)
    pallas_call x3, Pallas kernels, line_sum(): pl.pallas_call(line_sum_kernel, out_shape=jax.ShapeDtypeStruct(value.shap...  254 us
    pallas_call x1, Pallas kernels, attend_back(): pl.pallas_call(attend_back_kernel, out_shape=(jax.ShapeDtypeStruct((rows,...  60.6 us
    pallas_call x1, Pallas kernels, attend(): pl.pallas_call(attend_kernel, out_shape=(jax.ShapeDtypeStruct((rows, widt...  50.2 us
    ppermute x4, waiting for transfers between devices, swap_halves(): lax.ppermute(rows[half:], 'ctx', [(i, size - 1 - i) for i in range(size)])  29.6 us
    all_gather x1, waiting for transfers between devices, on_device(): lax.all_gather(jnp.concatenate([key_rows, value_rows], axis=1), 'ctx', ax...  23.2 us
    dot_general x6, matrix products, mat_product(): return jnp.dot(left_side, right_side, preferred_element_type=jnp.float32)  20.5 us
    dot_general x6, matrix products, left_product(): lax.dot_general(left_side, right_side, (((0,), (0,)), ((), ())), preferre...  18.4 us
    ppermute x10, waiting for transfers between devices, partner(): return lax.ppermute(value, 'ctx', [(i, i ^ distance) for i in range(size)])  17.7 us
  transfers between devices with their start and end apart: 22, of which 10 were waited for; matrix products, arithmetic and copies ran while one was open for 15% of the time, Pallas kernels for 37%

profile of v2, /device:TPU:0, one launch (start us, length us, event | category | flops | bytes accessed | tf_op | source)
XLA Modules:
  0.0 653.9 jit_solution(10418615322033827611)
XLA Ops:
  10.0 4.9 concatenate.43
  15.2 9.6 %all-reduce = bf16[5760]{0:T(1024)(128)(2,1)S(1)} all-reduce(bf16[5760]{0:T(1024)(128)(2,1)S(1)} %dynamic-update-slice), channel_id=2, replica_groups=mesh['fsdp'=2,'ctx'=4,'tp'=4] {'fsdp'}, use_global_device_ids=true, to_apply=%add | all-reduce | flops 5760 | bytes 23040
  30.8 10.7 %all_gather.23 = bf16[3,768,192]{1,2,0:T(8,128)(2,1)S(1)} all-gather(bf16[3,384,192]{1,2,0:T(8,128)(2,1)} %param.22), channel_id=1, replica_groups=mesh['fsdp'=2,'ctx'=4,'tp'=4] {'fsdp'}, dimensions={1}, use_global_device_ids=true | all-gather | bytes 1327104 | tf_op jit(solution)/shard_map/all_gather | solution.py:475
  53.2 13.0 %collective-permute-done = bf16[768,192]{1,0:T(8,128)(2,1)S(1)} collective-permute-done((bf16[768,192]{1,0:T(8,128)(2,1)S(1)}, bf16[768,192]{1,0:T(8,128)(2,1)S(1)}, u32[]{:S(2)}, u32[]{:S(2)}) %collective-permute-start) | collective-permute-done | bytes 294944 | tf_op jit(solution)/shard_map/ppermute | solution.py:397
  67.2 23.2 %all-gather.5.cloned.1.call-done.kv_ref = bf16[6144,384]{1,0:T(8,128)(2,1)} async-done(((bf16[1536,384]{1,0:T(8,128)(2,1)}), bf16[6144,384]{1,0:T(8,128)(2,1)}) %all-gather.5.cloned.1.call-update) | async-done | bytes 4718608 | tf_op jit(solution)/shard_map/all_gather | solution.py:507
  90.3 50.2 %shard_map.254 = (f32[1536,192]{1,0:T(8,128)}, bf16[3,1536,128]{2,1,0:T(8,128)(2,1)}) custom-call(s32[4]{0:T(128)} %pad_add_fusion.place_ref, bf16[1536,192]{1,0:T(8,128)(2,1)} %pad_maximum_fusion.3.q_ref, bf16[6144,384]{1,0:T(8,128)(2,1)} %all-gather.5.cloned.1.call-done.kv_ref), custom_call_target="tpu_custom_call" | custom-call | flops 14495514624 | bytes 8388608 | tf_op jit(solution)/shard_map/pallas_call | solution.py:347
  142.3 9.1 %all_gather.25 = bf16[192,768]{1,0:T(8,128)(2,1)S(1)} all-gather(bf16[192,384]{1,0:T(8,128)(2,1)S(1)} %copy-done.32), channel_id=1, replica_groups=mesh['fsdp'=2,'ctx'=4,'tp'=4] {'fsdp'}, dimensions={1}, use_global_device_ids=true | all-gather | bytes 442368 | tf_op jit(solution)/shard_map/all_gather | solution.py:498
  153.0 66.6 %shard_map.255 = bf16[1536,768]{1,0:T(8,128)(2,1)S(1)} custom-call(bf16[1536,768]{1,0:T(8,128)(2,1)S(1)} %convolution_convert_fusion.2.x_ref), custom_call_target="tpu_custom_call" | custom-call | flops 49999998976 | bytes 4194304 | tf_op jit(solution)/shard_map/pallas_call | solution.py:327
  221.7 7.0 %fusion.48 = f32[1536,768]{1,0:T(8,128)} fusion(bf16[768,768]{1,0:T(8,128)(2,1)} %all-gather.7.cloned.1.call-done, f32[768]{0:T(1024)S(1)} %add.217, f32[768]{0:T(1024)S(1)} %mul.181, f32[1536]{0:T(1024)S(1)} %fusion.42, bf16[1536,768]{1,0:T(8,128)(2,1)S(1)} %shard_map.255, bf16[1536,768]{1,0:T(8,128)(2,1)} %param.15, ...), kind=kOutput, calls=%fused_computation.151 | convolution fusion | flops 1822556160 | bytes 10638336 | tf_op jit(solution)/shard_map/dot_general | solution.py:26
  228.7 8.7 %convert_reduce_fusion.4 = (f32[768]{0:T(1024)}, bf16[1536,768]{1,0:T(8,128)(2,1)S(1)}) fusion(f32[1536,768]{1,0:T(8,128)} %fusion.48, f32[768]{0:T(1024)S(1)} %add.220, bf16[1536,768]{1,0:T(8,128)(2,1)} %param.16, bf16[768,768]{1,0:T(8,128)(2,1)} %all-gather.9.cloned.1.call-done), kind=kOutput, calls=%fused_computation.38 | convolution fusion | flops 1839070464 | bytes 10622976 | tf_op jit(solution)/shard_map/dot_general | solution.py:36
  240.8 63.9 %shard_map.256 = bf16[1536,768]{1,0:T(8,128)(2,1)S(1)} custom-call(bf16[1536,768]{1,0:T(8,128)(2,1)S(1)} %convolution_convert_fusion.x_ref), custom_call_target="tpu_custom_call" | custom-call | flops 49999998976 | bytes 4194304 | tf_op jit(solution)/shard_map/pallas_call | solution.py:327
  307.3 3.5 fusion.21
  310.8 3.4 convert_reduce_fusion.5
  315.1 8.9 %collective-permute-done.2 = bf16[768,192]{1,0:T(8,128)(2,1)S(1)} collective-permute-done((bf16[768,192]{1,0:T(8,128)(2,1)S(1)}, bf16[768,192]{1,0:T(8,128)(2,1)S(1)}, u32[]{:S(2)}, u32[]{:S(2)}) %collective-permute-start.2) | collective-permute-done | bytes 294944 | tf_op jit(solution)/shard_map/ppermute | solution.py:397
  325.0 60.6 %shard_map.257 = (bf16[1536,192]{1,0:T(8,128)(2,1)}, bf16[6144,384]{1,0:T(8,128)(2,1)}) custom-call(s32[4]{0:T(128)} %pad_add_fusion.place_ref, bf16[3,1536,128]{2,1,0:T(8,128)(2,1)} %get-tuple-element.19.qa_ref, bf16[1536,192]{1,0:T(8,128)(2,1)} %pad_maximum_fusion.5.go_ref, f32[1536,192]{1,0:T(8,128)} %get-tuple-element.18.out_ref, ...), custom_call_target="tpu_custom_call" | custom-call | flops 36238786560 | bytes 12582912 | tf_op jit(solution)/shard_map/pallas_call | solution.py:372
  385.9 5.8 convolution_convert_fusion.5
  404.1 4.2 collective-permute-start.13
  408.3 6.9 %convolution_convert_fusion.1 = bf16[1536,768]{1,0:T(8,128)(2,1)} fusion(bf16[768,768]{1,0:T(8,128)(2,1)S(1)} %copy-done.48, f32[1536,768]{1,0:T(8,128)} %fusion.48, f32[768]{0:T(1024)S(1)} %copy-done.47), kind=kOutput, calls=%fused_computation.49 | convolution fusion | flops 1824915456 | bytes 8260608 | tf_op jit(solution)/shard_map/dot_general | solution.py:26
  415.2 7.1 %collective-permute-done.13 = bf16[384,768]{1,0:T(8,128)(2,1)} collective-permute-done((bf16[384,768]{1,0:T(8,128)(2,1)}, bf16[384,768]{1,0:T(8,128)(2,1)}, u32[]{:S(2)}, u32[]{:S(2)}) %collective-permute-start.13) | collective-permute-done | bytes 589856 | tf_op jit(solution)/shard_map/ppermute | solution.py:441
  434.7 6.7 %collective-permute-done.14 = bf16[192,768]{1,0:T(8,128)(2,1)} collective-permute-done((bf16[192,768]{1,0:T(8,128)(2,1)}, bf16[192,768]{1,0:T(8,128)(2,1)}, u32[]{:S(2)}, u32[]{:S(2)}) %collective-permute-start.14) | collective-permute-done | bytes 294944 | tf_op jit(solution)/shard_map/ppermute | solution.py:403
  445.2 7.7 %collective-permute-done.3 = bf16[768,192]{1,0:T(8,128)(2,1)} collective-permute-done((bf16[768,192]{1,0:T(8,128)(2,1)}, bf16[768,192]{1,0:T(8,128)(2,1)}, u32[]{:S(2)}, u32[]{:S(2)}) %collective-permute-start.3) | collective-permute-done | bytes 294944 | tf_op jit(solution)/shard_map/ppermute | solution.py:397
  462.3 3.4 convolution_convert_fusion.8
  476.9 124.0 %shard_map.258 = bf16[1536,768]{1,0:T(8,128)(2,1)S(1)} custom-call(bf16[1536,768]{1,0:T(8,128)(2,1)S(1)} %add_convert_fusion.x_ref), custom_call_target="tpu_custom_call" | custom-call | flops 49999998976 | bytes 4194304 | tf_op jit(solution)/shard_map/pallas_call | solution.py:327
  610.3 11.1 %add_add_fusion.2 = (f32[1536,768]{1,0:T(8,128)}, bf16[1536,768]{1,0:T(8,128)(2,1)}, f32[768]{0:T(1024)}) fusion(bf16[1536,768]{1,0:T(8,128)(2,1)} %param.15, bf16[1536,768]{1,0:T(8,128)(2,1)} %copy-done.1, bf16[1536,768]{1,0:T(8,128)(2,1)} %param.16, f32[1536]{0:T(1024)} %negate_multiply_fusion, f32[1536]{0:T(1024)} %copy-done.40, f32[1536]{0:T(1024)} %copy-done.41, ...), kind=kLoop, calls=%fused_computation.40 | loop fusion | flops 33029376 | bytes 21298176 | tf_op jit(solution)/shard_map/add | solution.py:569
  (258 shorter events, 118.0 us)
Async XLA Ops:
  7.2 83.2 %all-gather.5.cloned.1.call-start = ((), (), s32[]{:S(2)}) async-start(), calls=%async_computation.1 | async-start | bytes 5898240 | tf_op jit(solution)/shard_map/all_gather | solution.py:507
  49.3 172.4 %all-gather.7.cloned.1.call-start = ((), (), s32[]{:S(2)}) async-start(), calls=%async_computation.2 | async-start | bytes 1769472 | tf_op jit(solution)/shard_map/all_gather | solution.py:499
  51.9 14.2 %collective-permute-start = (bf16[768,192]{1,0:T(8,128)(2,1)S(1)}, bf16[768,192]{1,0:T(8,128)(2,1)S(1)}, u32[]{:S(2)}, u32[]{:S(2)}) collective-permute-start(bf16[768,192]{1,0:T(8,128)(2,1)S(1)} %get-tuple-element.113), channel_id=1, source_target_pairs={{0,12},{4,8},{8,4},{12,0},{1,13},{5,9},{9,5},{13,1},{2,14},{6,10},... | collective-permute-start | bytes 884744 | tf_op jit(solution)/shard_map/ppermute | solution.py:397
  52.1 176.6 %all-gather.9.cloned.1.call-start = ((), (), s32[]{:S(2)}) async-start(), calls=%async_computation.3 | async-start | bytes 1769472 | tf_op jit(solution)/shard_map/all_gather | solution.py:500
  142.1 9.4 %collective-permute-start.1 = (bf16[768,192]{1,0:T(8,128)(2,1)S(1)}, bf16[768,192]{1,0:T(8,128)(2,1)S(1)}, u32[]{:S(2)}, u32[]{:S(2)}) collective-permute-start(bf16[768,192]{1,0:T(8,128)(2,1)S(1)} %get-tuple-element.111), channel_id=1, source_target_pairs={{0,12},{4,8},{8,4},{12,0},{1,13},{5,9},{9,5},{13,1},{2,14},{6,10},... | collective-permute-start | bytes 884744 | tf_op jit(solution)/shard_map/ppermute | solution.py:397
  142.2 320.1 %reduce-scatter.2.cloned.1.call-start = ((), (), s32[]{:S(2)}) async-start(), calls=%async_computation.5 | async-start | bytes 5898240 | tf_op jit(solution)/shard_map/reduce_scatter | solution.py:558
  142.2 249.5 %copy-start.31 = (f32[768]{0:T(1024)}, f32[768]{0:T(1024)S(1)}, u32[]{:S(2)}) copy-start(f32[768]{0:T(1024)S(1)} %add.213) | copy-start | bytes 9220
  142.3 249.5 %copy-start.39 = (f32[768]{0:T(1024)}, f32[768]{0:T(1024)S(1)}, u32[]{:S(2)}) copy-start(f32[768]{0:T(1024)S(1)} %mul.181) | copy-start | bytes 9220
  315.0 9.0 %collective-permute-start.2 = (bf16[768,192]{1,0:T(8,128)(2,1)S(1)}, bf16[768,192]{1,0:T(8,128)(2,1)S(1)}, u32[]{:S(2)}, u32[]{:S(2)}) collective-permute-start(bf16[768,192]{1,0:T(8,128)(2,1)S(1)} %get-tuple-element.109), channel_id=1, source_target_pairs={{0,12},{4,8},{8,4},{12,0},{1,13},{5,9},{9,5},{13,1},{2,14},{6,10},... | collective-permute-start | bytes 884744 | tf_op jit(solution)/shard_map/ppermute | solution.py:397
  385.6 224.7 %all-reduce.3.cloned.1.call-start = ((), (), s32[]{:S(2)}) async-start(), calls=%async_computation.4 | async-start | bytes 4718592 | tf_op jit(solution)/shard_map/psum | solution.py:532
  396.3 4.7 collective-permute-start.12
  404.1 18.3 %collective-permute-start.13 = (bf16[384,768]{1,0:T(8,128)(2,1)}, bf16[384,768]{1,0:T(8,128)(2,1)}, u32[]{:S(2)}, u32[]{:S(2)}) collective-permute-start(bf16[384,768]{1,0:T(8,128)(2,1)} %dynamic-slice_bitcast_fusion.1), channel_id=1, source_target_pairs={{0,16},{16,0},{1,17},{17,1},{2,18},{18,2},{3,19},{19,3},{4,20},{20... | collective-permute-start | bytes 1769480 | tf_op jit(solution)/shard_map/ppermute | solution.py:441
  424.4 17.0 %collective-permute-start.14 = (bf16[192,768]{1,0:T(8,128)(2,1)}, bf16[192,768]{1,0:T(8,128)(2,1)}, u32[]{:S(2)}, u32[]{:S(2)}) collective-permute-start(bf16[192,768]{1,0:T(8,128)(2,1)} %dynamic-slice_bitcast_fusion.2), channel_id=1, source_target_pairs={{0,8},{4,12},{8,0},{12,4},{1,9},{5,13},{9,1},{13,5},{2,10},{6,14},... | collective-permute-start | bytes 884744 | tf_op jit(solution)/shard_map/ppermute | solution.py:403
  429.0 24.0 %collective-permute-start.3 = (bf16[768,192]{1,0:T(8,128)(2,1)}, bf16[768,192]{1,0:T(8,128)(2,1)}, u32[]{:S(2)}, u32[]{:S(2)}) collective-permute-start(bf16[768,192]{1,0:T(8,128)(2,1)} %get-tuple-element.107), channel_id=1, source_target_pairs={{0,12},{4,8},{8,4},{12,0},{1,13},{5,9},{9,5},{13,1},{2,14},{6,10},... | collective-permute-start | bytes 884744 | tf_op jit(solution)/shard_map/ppermute | solution.py:397
  443.2 16.4 %collective-permute-start.15 = (bf16[192,768]{1,0:T(8,128)(2,1)}, bf16[192,768]{1,0:T(8,128)(2,1)}, u32[]{:S(2)}, u32[]{:S(2)}) collective-permute-start(bf16[192,768]{1,0:T(8,128)(2,1)} %fusion.38), channel_id=1, source_target_pairs={{0,8},{4,12},{8,0},{12,4},{1,9},{5,13},{9,1},{13,5},{2,10},{6,14},... | collective-permute-start | bytes 884744 | tf_op jit(solution)/shard_map/ppermute | solution.py:403
  462.3 165.9 %collective-permute-start.16 = (bf16[384,768]{1,0:T(8,128)(2,1)}, bf16[384,768]{1,0:T(8,128)(2,1)}, u32[]{:S(2)}, u32[]{:S(2)}) collective-permute-start(bf16[384,768]{1,0:T(8,128)(2,1)} %pad_maximum_fusion.7), channel_id=1, source_target_pairs={{0,4},{4,0},{8,12},{12,8},{1,5},{5,1},{9,13},{13,9},{2,6},{6,2},{1... | collective-permute-start | bytes 1769480 | tf_op jit(solution)/shard_map/ppermute | solution.py:403
  472.9 134.2 %collective-permute-start.7 = (bf16[2,768,192]{1,2,0:T(8,128)(2,1)S(1)}, bf16[2,768,192]{1,2,0:T(8,128)(2,1)S(1)}, u32[]{:S(2)}, u32[]{:S(2)}) collective-permute-start(bf16[2,768,192]{1,2,0:T(8,128)(2,1)S(1)} %bitcast.112), channel_id=1, source_target_pairs={{0,4},{4,0},{8,12},{12,8},{1,5},{5,1},{9,13},{13,9},{2,6},{6,2},{1... | collective-permute-start | bytes 1769480 | tf_op jit(solution)/shard_map/ppermute | solution.py:403
  608.8 16.1 %collective-permute-start.8 = (bf16[768,192]{0,1:T(8,128)(2,1)}, bf16[768,192]{0,1:T(8,128)(2,1)}, u32[]{:S(2)}, u32[]{:S(2)}) collective-permute-start(bf16[768,192]{0,1:T(8,128)(2,1)} %dynamic-slice_bitcast_fusion.3), channel_id=1, source_target_pairs={{0,16},{16,0},{1,17},{17,1},{2,18},{18,2},{3,19},{19,3},{4,20},{20... | collective-permute-start | bytes 884744 | tf_op jit(solution)/shard_map/ppermute | solution.py:441
  624.8 4.8 collective-permute-start.4
  626.7 6.6 %collective-permute-start.9 = (bf16[384,192]{0,1:T(8,128)(2,1)S(1)}, bf16[384,192]{0,1:T(8,128)(2,1)S(1)}, u32[]{:S(2)}, u32[]{:S(2)}) collective-permute-start(bf16[384,192]{0,1:T(8,128)(2,1)S(1)} %bitcast.117), channel_id=1, source_target_pairs={{0,8},{4,12},{8,0},{12,4},{1,9},{5,13},{9,1},{13,5},{2,10},{6,14},... | collective-permute-start | bytes 442376 | tf_op jit(solution)/shard_map/ppermute | solution.py:403
  629.7 5.3 collective-permute-start.5
  633.3 5.3 collective-permute-start.10
  635.6 6.3 collective-permute-start.6
  639.4 4.8 collective-permute-start.11
  (51 other events, 1295.8 us)
Sparse Core Ops, SparseCore 0:
  49.4 40.9 all-gather.4
  91.9 22.2 all-gather.6
  142.3 26.5 all-gather.8
  385.7 64.6 reduce-scatter.1
  452.8 136.5 all-reduce.2

commit v3 on v2

--- a/solution.py
+++ b/solution.py
@@ -231,7 +231,7 @@
 LINE_STEPS = 12
 
 
-def line_sum_kernel(x_ref, out_ref, land, cross, part, send_e, recv_e, send_c, recv_c):
+def line_sum_kernel(x_ref, after_ref, out_ref, land, cross, part, send_e, recv_e, send_c, recv_c):
     me = lax.axis_index("tp")
     edge_peer = me + 1 - 2 * (me % 2)
     cross_peer = 3 - me
@@ -319,7 +319,7 @@
             edge_copy(c, out_ref).wait_send()
 
 
-def line_sum(value, call):
+def line_sum(value, call, after):
     if lax.axis_size("tp") != 4 or value.shape[0] % (16 * LINE_STEPS) != 0:
         return lax.psum(value, "tp")
     buffer = pltpu.VMEM(value.shape, value.dtype)
@@ -327,7 +327,7 @@
     return pl.pallas_call(
         line_sum_kernel,
         out_shape=jax.ShapeDtypeStruct(value.shape, value.dtype),
-        in_specs=in_vmem(1),
+        in_specs=in_vmem(1) + [pl.BlockSpec(memory_space=pl.ANY)],
         out_specs=in_vmem(1)[0],
         scratch_shapes=[buffer, buffer, buffer, sems, sems, sems, sems],
         compiler_params=pltpu.CompilerParams(
@@ -336,7 +336,7 @@
         cost_estimate=pl.CostEstimate(
             flops=50_000_000_000, bytes_accessed=4 << 20, transcendentals=0
         ),
-    )(value)
+    )(value, after)
 
 
 def attend(place, queries, kv_all):
@@ -428,6 +428,20 @@
     if lax.axis_size("fsdp") == 2:
         return vector + lax.ppermute(vector, "fsdp", [(0, 1), (1, 0)])
     return lax.psum(vector, "fsdp")
+
+
+def scatter_blocks(terms, zero):
+    size = lax.axis_size("ctx")
+    rows, width = terms.shape[0] // size, terms.shape[1]
+    block = terms.reshape(size, rows, width)
+    for i in range(size.bit_length() - 1):
+        bit = (lax.axis_index("ctx") // (1 << i)) % 2
+        split = block.reshape(block.shape[0] // 2, 2, rows, width)
+        keep = lax.dynamic_index_in_dim(split, bit, 1, keepdims=False)
+        send = lax.dynamic_index_in_dim(split, 1 - bit, 1, keepdims=False)
+        got = partner(send, 1 << i).astype(jnp.float32) + zero
+        block = (keep.astype(jnp.float32) + got).astype(jnp.bfloat16)
+    return block.reshape(rows, width)
 
 
 def reduce_shards(block):
@@ -517,7 +531,7 @@
     attended = swap_halves(attn_out.astype(jnp.bfloat16))
     attn_partial = mat_product(attended, out_full)
     residual = (
-        tokens_f + line_sum(attn_partial.astype(jnp.bfloat16), 0).astype(jnp.float32) + out_shift
+        tokens_f + line_sum(attn_partial.astype(jnp.bfloat16), 0, attended).astype(jnp.float32) + out_shift
     )
     normed_two = layer_norm(residual, gain_two, shift_two).astype(jnp.bfloat16)
     hidden = mat_product(normed_two, in_full) + in_shift
@@ -526,11 +540,10 @@
     grad_active = right_product(cotangent, back_full)
     grad_hidden = gelu_pull(grad_active)[0].astype(jnp.bfloat16)
     norm_two_partial = right_product(grad_hidden, in_full)
-    grad_normed_two = line_sum(norm_two_partial.astype(jnp.bfloat16), 1).astype(jnp.float32)
+    grad_normed_two = line_sum(norm_two_partial.astype(jnp.bfloat16), 1, active).astype(jnp.float32)
+    grad_normed_two, active = lax.optimization_barrier((grad_normed_two, active))
     ff_partial = mat_product(active, back_full)
-    mixed = (
-        residual + lax.psum(ff_partial.astype(jnp.bfloat16), "tp").astype(jnp.float32) + back_shift
-    ).astype(jnp.bfloat16)
+    ff_total = lax.psum(ff_partial.astype(jnp.bfloat16), "tp")
     back_shift_grad = column_sums(cotangent)
     back_grad = left_product(cotangent, active).astype(jnp.bfloat16)
     in_shift_grad = column_sums(grad_hidden)
@@ -554,8 +567,10 @@
     out_grad = left_product(grad_attn, attended).astype(jnp.bfloat16)
     grad_swapped = swap_halves(grad_attended)
     grad_queries, kv_terms = attend_back(place, queries_wide, grad_swapped, attn_out, kv_all)
+    residual_late, unused = lax.optimization_barrier((residual, grad_queries))
+    mixed = (residual_late + ff_total.astype(jnp.float32) + back_shift).astype(jnp.bfloat16)
     grad_queries = swap_halves(grad_queries)
-    grad_kv = lax.psum_scatter(kv_terms, "ctx", scatter_dimension=0, tiled=True)
+    grad_kv = scatter_blocks(kv_terms, ff_total[0, 0].astype(jnp.float32) * 0.0)
     grad_keys = grad_kv[:, :local_width]
     grad_values = grad_kv[:, local_width:]
     norm_one_partial = (
@@ -563,7 +578,7 @@
         + right_product(grad_keys, qkv_full[1])
         + right_product(grad_values, qkv_full[2])
     )
-    grad_normed_one = line_sum(norm_one_partial.astype(jnp.bfloat16), 2).astype(jnp.float32)
+    grad_normed_one = line_sum(norm_one_partial.astype(jnp.bfloat16), 2, mixed).astype(jnp.float32)
     unused, first_pull = jax.vjp(layer_norm, tokens_f, gain_one, shift_one)
     grad_tokens, gain_one_grad, shift_one_grad = first_pull(grad_normed_one)
     input_rows = grad_residual + grad_tokens

time: 659 us -> 592 us (0.90)
  Pallas kernels: 365 us -> 302 us
    pallas_call x3, Pallas kernels: 254 us -> 191 us  [line_sum(): pl.pallas_call(line_sum_kernel, out_shape=jax.ShapeDtypeStruct(value.shap...]
    add x1 -> x0, other arithmetic: 11.1 us -> none  [on_device(): input_rows = grad_residual + grad_tokens]
    ppermute x4, waiting for transfers between devices: 29.6 us -> 19.3 us  [swap_halves(): lax.ppermute(rows[half:], 'ctx', [(i, size - 1 - i) for i in range(size)])]
    convert_element_type x0 -> x4, other arithmetic: none -> 9.38 us  [the longest x1 3.83 us: on_device(): (residual_late + ff_total.astype(jnp.float32) + back_shift).astype(jnp.bf...]
    ppermute x10 -> x12, waiting for transfers between devices: 17.7 us -> 25.2 us  [partner(): return lax.ppermute(value, 'ctx', [(i, i ^ distance) for i in range(size)])]
    ppermute x2, waiting for transfers between devices: 7.11 us -> 13.9 us  [reduce_shards(): got = lax.ppermute(send, 'fsdp', [(0, 1), (1, 0)])]
    dot_general x6, matrix products: 18.4 us -> 11.8 us  [left_product(): lax.dot_general(left_side, right_side, (((0,), (0,)), ((), ())), preferre...]
  transfers between devices with their start and end apart: 22 -> 23, of which waited for: 10 -> 10; matrix products, arithmetic and copies ran while one was open for 15% -> 15% of each run, Pallas kernels for 37% -> 41%
where the time goes in v3:
time: 592 us; the launch traced here: 581 us
  Pallas kernels  302 us (51%)
  waiting for transfers between devices  81.7 us (14%)
  other arithmetic  53.9 us (9%)
  matrix products  48.6 us (8%)
  local copies, waits for them, and re-layouts  41.1 us (7%)
  blocking collectives  26.3 us (4%)
  between operations  16.5 us (3%)
  starting transfers between devices  10.8 us (2%)
    pallas_call x3, Pallas kernels, line_sum(): pl.pallas_call(line_sum_kernel, out_shape=jax.ShapeDtypeStruct(value.shap...  191 us
    pallas_call x1, Pallas kernels, attend_back(): pl.pallas_call(attend_back_kernel, out_shape=(jax.ShapeDtypeStruct((rows,...  60.7 us
    pallas_call x1, Pallas kernels, attend(): pl.pallas_call(attend_kernel, out_shape=(jax.ShapeDtypeStruct((rows, widt...  50.1 us
    ppermute x12, waiting for transfers between devices, partner(): return lax.ppermute(value, 'ctx', [(i, i ^ distance) for i in range(size)])  25.2 us
    all_gather x1, waiting for transfers between devices, on_device(): lax.all_gather(jnp.concatenate([key_rows, value_rows], axis=1), 'ctx', ax...  23.2 us
    dot_general x6, matrix products, right_product(): lax.dot_general(left_side, right_side, (((1,), (1,)), ((), ())), preferre...  19.6 us
    ppermute x4, waiting for transfers between devices, swap_halves(): lax.ppermute(rows[half:], 'ctx', [(i, size - 1 - i) for i in range(size)])  19.3 us
    dot_general x6, matrix products, mat_product(): return jnp.dot(left_side, right_side, preferred_element_type=jnp.float32)  17.2 us
  transfers between devices with their start and end apart: 23, of which 10 were waited for; matrix products, arithmetic and copies ran while one was open for 15% of the time, Pallas kernels for 41%

profile of v3, /device:TPU:0, one launch (start us, length us, event | category | flops | bytes accessed | tf_op | source)
XLA Modules:
  0.0 581.0 jit_solution(7014131883302183221)
XLA Ops:
  10.0 4.9 concatenate.43
  15.2 9.6 %all-reduce = bf16[5760]{0:T(1024)(128)(2,1)S(1)} all-reduce(bf16[5760]{0:T(1024)(128)(2,1)S(1)} %dynamic-update-slice), channel_id=2, replica_groups=mesh['fsdp'=2,'ctx'=4,'tp'=4] {'fsdp'}, use_global_device_ids=true, to_apply=%add | all-reduce | flops 5760 | bytes 23040
  29.0 10.7 %all_gather.23 = bf16[3,768,192]{1,2,0:T(8,128)(2,1)S(1)} all-gather(bf16[3,384,192]{1,2,0:T(8,128)(2,1)} %param.22), channel_id=1, replica_groups=mesh['fsdp'=2,'ctx'=4,'tp'=4] {'fsdp'}, dimensions={1}, use_global_device_ids=true | all-gather | bytes 1327104 | tf_op jit(solution)/shard_map/all_gather | solution.py:489
  55.9 11.3 %collective-permute-done = bf16[768,192]{1,0:T(8,128)(2,1)S(1)} collective-permute-done((bf16[768,192]{1,0:T(8,128)(2,1)S(1)}, bf16[768,192]{1,0:T(8,128)(2,1)S(1)}, u32[]{:S(2)}, u32[]{:S(2)}) %collective-permute-start) | collective-permute-done | bytes 294944 | tf_op jit(solution)/shard_map/ppermute | solution.py:397
  68.2 23.2 %all-gather.5.cloned.1.call-done.kv_ref = bf16[6144,384]{1,0:T(8,128)(2,1)} async-done(((bf16[1536,384]{1,0:T(8,128)(2,1)}), bf16[6144,384]{1,0:T(8,128)(2,1)}) %all-gather.5.cloned.1.call-update) | async-done | bytes 4718608 | tf_op jit(solution)/shard_map/all_gather | solution.py:521
  91.4 50.1 %shard_map.254 = (f32[1536,192]{1,0:T(8,128)}, bf16[3,1536,128]{2,1,0:T(8,128)(2,1)}) custom-call(s32[4]{0:T(128)} %pad_add_fusion.place_ref, bf16[1536,192]{1,0:T(8,128)(2,1)} %pad_maximum_fusion.3.q_ref, bf16[6144,384]{1,0:T(8,128)(2,1)} %all-gather.5.cloned.1.call-done.kv_ref), custom_call_target="tpu_custom_call" | custom-call | flops 14495514624 | bytes 8388608 | tf_op jit(solution)/shard_map/pallas_call | solution.py:347
  145.0 6.0 %all_gather.25 = bf16[192,768]{1,0:T(8,128)(2,1)S(1)} all-gather(bf16[192,384]{1,0:T(8,128)(2,1)} %param.24), channel_id=1, replica_groups=mesh['fsdp'=2,'ctx'=4,'tp'=4] {'fsdp'}, dimensions={1}, use_global_device_ids=true | all-gather | bytes 442368 | tf_op jit(solution)/shard_map/all_gather | solution.py:512
  152.8 64.8 %shard_map.255 = bf16[1536,768]{1,0:T(8,128)(2,1)S(1)} custom-call(bf16[1536,768]{1,0:T(8,128)(2,1)S(1)} %convolution_convert_fusion.2.x_ref, bf16[1536,192]{1,0:T(8,128)(2,1)S(1)} %pad_maximum_fusion.4.after_ref), custom_call_target="tpu_custom_call" | custom-call | flops 49999998976 | bytes 4194304 | tf_op jit(solution)/shard_map/pallas_call | solution.py:327
  222.7 6.3 %fusion.54 = f32[1536,768]{1,0:T(8,128)} fusion(bf16[1536,768]{1,0:T(8,128)(2,1)} %add_convert_fusion.2, bf16[768,768]{1,0:T(8,128)(2,1)} %all-gather.9.cloned.1.call-done), kind=kOutput, calls=%fused_computation.157 | convolution fusion | flops 1811939328 | bytes 8257536 | tf_op jit(solution)/shard_map/dot_general | solution.py:26
  229.0 7.5 %convert_reduce_fusion.3 = (f32[768]{0:T(1024)}, bf16[1536,768]{1,0:T(8,128)(2,1)S(1)}, bf16[1536,768]{1,0:T(8,128)(2,1)S(1)}) fusion(f32[1536,768]{1,0:T(8,128)} %fusion.54, f32[768]{0:T(1024)S(1)} %copy-done.55, bf16[1536,768]{1,0:T(8,128)(2,1)S(1)} %copy-done.7, bf16[768,768]{1,0:T(8,128)(2,1)} %all-gather.7.cloned.1.call-done), kind=kOutput, calls=%fused_computation.33 | convolution fusion | flops 1841429760 | bytes 12982272 | tf_op jit(solution)/shard_map/dot_general | solution.py:36
  240.7 61.9 %shard_map.256 = bf16[1536,768]{1,0:T(8,128)(2,1)S(1)} custom-call(bf16[1536,768]{1,0:T(8,128)(2,1)S(1)} %convolution_convert_fusion.1.x_ref, bf16[1536,768]{1,0:T(8,128)(2,1)S(1)} %get-tuple-element.26.after_ref), custom_call_target="tpu_custom_call" | custom-call | flops 49999998976 | bytes 4194304 | tf_op jit(solution)/shard_map/pallas_call | solution.py:327
  305.9 3.5 fusion.44
  312.5 3.4 convolution_convert_fusion
  315.9 3.1 convert_reduce_fusion.4
  323.7 7.1 %collective-permute-done.2 = bf16[768,192]{1,0:T(8,128)(2,1)S(1)} collective-permute-done((bf16[768,192]{1,0:T(8,128)(2,1)S(1)}, bf16[768,192]{1,0:T(8,128)(2,1)S(1)}, u32[]{:S(2)}, u32[]{:S(2)}) %collective-permute-start.2) | collective-permute-done | bytes 294944 | tf_op jit(solution)/shard_map/ppermute | solution.py:397
  331.9 60.7 %shard_map.257 = (bf16[1536,192]{1,0:T(8,128)(2,1)}, bf16[6144,384]{1,0:T(8,128)(2,1)}) custom-call(s32[4]{0:T(128)} %pad_add_fusion.place_ref, bf16[3,1536,128]{2,1,0:T(8,128)(2,1)} %get-tuple-element.22.qa_ref, bf16[1536,192]{1,0:T(8,128)(2,1)} %pad_maximum_fusion.5.go_ref, f32[1536,192]{1,0:T(8,128)} %get-tuple-element.21.out_ref, ...), custom_call_target="tpu_custom_call" | custom-call | flops 36238786560 | bytes 12582912 | tf_op jit(solution)/shard_map/pallas_call | solution.py:372
  392.6 3.4 dynamic-slice_bitcast_fusion
  401.0 12.3 %collective-permute-done.15 = bf16[384,768]{1,0:T(8,128)(2,1)S(1)} collective-permute-done((bf16[384,768]{1,0:T(8,128)(2,1)S(1)}, bf16[384,768]{1,0:T(8,128)(2,1)S(1)}, u32[]{:S(2)}, u32[]{:S(2)}) %collective-permute-start.15) | collective-permute-done | bytes 589856 | tf_op jit(solution)/shard_map/ppermute | solution.py:455
  436.7 3.8 add_convert_fusion.1.after_ref
  440.5 18.7 %collective-permute-done.5 = bf16[1,1536,384]{2,1,0:T(8,128)(2,1)} collective-permute-done((bf16[1,1536,384]{2,1,0:T(8,128)(2,1)S(1)}, bf16[1,1536,384]{2,1,0:T(8,128)(2,1)}, u32[]{:S(2)}, u32[]{:S(2)}) %collective-permute-start.5) | collective-permute-done | bytes 1179680 | tf_op jit(solution)/shard_map/ppermute | solution.py:403
  470.3 3.2 reshape.228
  475.9 3.4 add_convert_fusion.x_ref
  479.3 64.8 %shard_map.258 = bf16[1536,768]{1,0:T(8,128)(2,1)S(1)} custom-call(bf16[1536,768]{1,0:T(8,128)(2,1)S(1)} %add_convert_fusion.x_ref, bf16[1536,768]{1,0:T(8,128)(2,1)S(1)} %add_convert_fusion.1.after_ref), custom_call_target="tpu_custom_call" | custom-call | flops 49999998976 | bytes 4194304 | tf_op jit(solution)/shard_map/pallas_call | solution.py:327
  550.3 3.9 convert_reduce_fusion.2
  (290 shorter events, 117.0 us)
Async XLA Ops:
  7.2 84.2 %all-gather.5.cloned.1.call-start = ((), (), s32[]{:S(2)}) async-start(), calls=%async_computation | async-start | bytes 5898240 | tf_op jit(solution)/shard_map/all_gather | solution.py:521
  50.3 172.4 %all-gather.9.cloned.1.call-start = ((), (), s32[]{:S(2)}) async-start(), calls=%async_computation.2 | async-start | bytes 1769472 | tf_op jit(solution)/shard_map/all_gather | solution.py:513
  53.0 14.2 %collective-permute-start = (bf16[768,192]{1,0:T(8,128)(2,1)S(1)}, bf16[768,192]{1,0:T(8,128)(2,1)S(1)}, u32[]{:S(2)}, u32[]{:S(2)}) collective-permute-start(bf16[768,192]{1,0:T(8,128)(2,1)S(1)} %get-tuple-element.122), channel_id=1, source_target_pairs={{0,12},{4,8},{8,4},{12,0},{1,13},{5,9},{9,5},{13,1},{2,14},{6,10},... | collective-permute-start | bytes 884744 | tf_op jit(solution)/shard_map/ppermute | solution.py:397
  53.1 176.0 %all-gather.7.cloned.1.call-start = ((), (), s32[]{:S(2)}) async-start(), calls=%async_computation.1 | async-start | bytes 1769472 | tf_op jit(solution)/shard_map/all_gather | solution.py:514
  143.0 8.9 %collective-permute-start.1 = (bf16[768,192]{1,0:T(8,128)(2,1)S(1)}, bf16[768,192]{1,0:T(8,128)(2,1)S(1)}, u32[]{:S(2)}, u32[]{:S(2)}) collective-permute-start(bf16[768,192]{1,0:T(8,128)(2,1)S(1)} %get-tuple-element.120), channel_id=1, source_target_pairs={{0,12},{4,8},{8,4},{12,0},{1,13},{5,9},{9,5},{13,1},{2,14},{6,10},... | collective-permute-start | bytes 884744 | tf_op jit(solution)/shard_map/ppermute | solution.py:397
  143.1 282.4 %all-reduce.3.cloned.1.call-start = ((), (), s32[]{:S(2)}) async-start(), calls=%async_computation.3 | async-start | bytes 4718592 | tf_op jit(solution)/shard_map/psum | solution.py:546
  320.6 10.3 %collective-permute-start.2 = (bf16[768,192]{1,0:T(8,128)(2,1)S(1)}, bf16[768,192]{1,0:T(8,128)(2,1)S(1)}, u32[]{:S(2)}, u32[]{:S(2)}) collective-permute-start(bf16[768,192]{1,0:T(8,128)(2,1)S(1)} %get-tuple-element.118), channel_id=1, source_target_pairs={{0,12},{4,8},{8,4},{12,0},{1,13},{5,9},{9,5},{13,1},{2,14},{6,10},... | collective-permute-start | bytes 884744 | tf_op jit(solution)/shard_map/ppermute | solution.py:397
  322.0 73.9 %collective-permute-start.14 = (bf16[2,384,768]{2,1,0:T(8,128)(2,1)S(1)}, bf16[2,384,768]{2,1,0:T(8,128)(2,1)}, u32[]{:S(2)}, u32[]{:S(2)}) collective-permute-start(bf16[2,384,768]{2,1,0:T(8,128)(2,1)S(1)} %dynamic-slice_bitcast_fusion.1), channel_id=1, source_target_pairs={{0,4},{4,0},{8,12},{12,8},{1,5},{5,1},{9,13},{13,9},{2,6},{6,2},{1... | collective-permute-start | bytes 3538952 | tf_op jit(solution)/shard_map/ppermute | solution.py:403
  395.9 31.4 %collective-permute-start.4 = (bf16[2,1536,384]{2,1,0:T(8,128)(2,1)}, bf16[2,1536,384]{2,1,0:T(8,128)(2,1)}, u32[]{:S(2)}, u32[]{:S(2)}) collective-permute-start(bf16[2,1536,384]{2,1,0:T(8,128)(2,1)} %dynamic-slice_bitcast_fusion), channel_id=1, source_target_pairs={{0,4},{4,0},{8,12},{12,8},{1,5},{5,1},{9,13},{13,9},{2,6},{6,2},{1... | collective-permute-start | bytes 7077896 | tf_op jit(solution)/shard_map/ppermute | solution.py:403
  397.5 15.8 %collective-permute-start.15 = (bf16[384,768]{1,0:T(8,128)(2,1)S(1)}, bf16[384,768]{1,0:T(8,128)(2,1)S(1)}, u32[]{:S(2)}, u32[]{:S(2)}) collective-permute-start(bf16[384,768]{1,0:T(8,128)(2,1)S(1)} %dynamic-slice_bitcast_fusion.2), channel_id=1, source_target_pairs={{0,16},{16,0},{1,17},{17,1},{2,18},{18,2},{3,19},{19,3},{4,20},{20... | collective-permute-start | bytes 1769480 | tf_op jit(solution)/shard_map/ppermute | solution.py:455
  401.0 19.1 %collective-permute-start.3 = (bf16[768,192]{1,0:T(8,128)(2,1)}, bf16[768,192]{1,0:T(8,128)(2,1)}, u32[]{:S(2)}, u32[]{:S(2)}) collective-permute-start(bf16[768,192]{1,0:T(8,128)(2,1)} %get-tuple-element.116), channel_id=1, source_target_pairs={{0,12},{4,8},{8,4},{12,0},{1,13},{5,9},{9,5},{13,1},{2,14},{6,10},... | collective-permute-start | bytes 884744 | tf_op jit(solution)/shard_map/ppermute | solution.py:397
  415.1 8.9 %collective-permute-start.16 = (bf16[192,768]{1,0:T(8,128)(2,1)}, bf16[192,768]{1,0:T(8,128)(2,1)S(1)}, u32[]{:S(2)}, u32[]{:S(2)}) collective-permute-start(bf16[192,768]{1,0:T(8,128)(2,1)} %dynamic-slice_bitcast_fusion.3), channel_id=1, source_target_pairs={{0,8},{4,12},{8,0},{12,4},{1,9},{5,13},{9,1},{13,5},{2,10},{6,14},... | collective-permute-start | bytes 884744 | tf_op jit(solution)/shard_map/ppermute | solution.py:403
  425.1 10.5 %collective-permute-start.17 = (bf16[192,768]{1,0:T(8,128)(2,1)S(1)}, bf16[192,768]{1,0:T(8,128)(2,1)S(1)}, u32[]{:S(2)}, u32[]{:S(2)}) collective-permute-start(bf16[192,768]{1,0:T(8,128)(2,1)S(1)} %fusion.34), channel_id=1, source_target_pairs={{0,8},{4,12},{8,0},{12,4},{1,9},{5,13},{9,1},{13,5},{2,10},{6,14},... | collective-permute-start | bytes 884744 | tf_op jit(solution)/shard_map/ppermute | solution.py:403
  432.0 27.2 %collective-permute-start.5 = (bf16[1,1536,384]{2,1,0:T(8,128)(2,1)S(1)}, bf16[1,1536,384]{2,1,0:T(8,128)(2,1)}, u32[]{:S(2)}, u32[]{:S(2)}) collective-permute-start(bf16[1,1536,384]{2,1,0:T(8,128)(2,1)S(1)} %constant_dynamic-slice_fusion.3), channel_id=1, source_target_pairs={{0,8},{4,12},{8,0},{12,4},{1,9},{5,13},{9,1},{13,5},{2,10},{6,14},... | collective-permute-start | bytes 3538952 | tf_op jit(solution)/shard_map/ppermute | solution.py:403
  436.7 121.7 %collective-permute-start.18 = (bf16[384,768]{1,0:T(8,128)(2,1)}, bf16[384,768]{1,0:T(8,128)(2,1)}, u32[]{:S(2)}, u32[]{:S(2)}) collective-permute-start(bf16[384,768]{1,0:T(8,128)(2,1)} %pad_maximum_fusion.7), channel_id=1, source_target_pairs={{0,4},{4,0},{8,12},{12,8},{1,5},{5,1},{9,13},{13,9},{2,6},{6,2},{1... | collective-permute-start | bytes 1769480 | tf_op jit(solution)/shard_map/ppermute | solution.py:403
  475.8 72.9 %collective-permute-start.9 = (bf16[2,768,192]{1,2,0:T(8,128)(2,1)S(1)}, bf16[2,768,192]{1,2,0:T(8,128)(2,1)S(1)}, u32[]{:S(2)}, u32[]{:S(2)}) collective-permute-start(bf16[2,768,192]{1,2,0:T(8,128)(2,1)S(1)} %bitcast.131), channel_id=1, source_target_pairs={{0,4},{4,0},{8,12},{12,8},{1,5},{5,1},{9,13},{13,9},{2,6},{6,2},{1... | collective-permute-start | bytes 1769480 | tf_op jit(solution)/shard_map/ppermute | solution.py:403
  479.3 64.9 %copy-start.3 = (bf16[1536,768]{1,0:T(8,128)(2,1)S(1)}, bf16[1536,768]{1,0:T(8,128)(2,1)}, u32[]{:S(2)}) copy-start(bf16[1536,768]{1,0:T(8,128)(2,1)} %param.15) | copy-start | bytes 7077892
  548.9 7.6 %collective-permute-start.10 = (bf16[768,192]{0,1:T(8,128)(2,1)S(1)}, bf16[768,192]{0,1:T(8,128)(2,1)S(1)}, u32[]{:S(2)}, u32[]{:S(2)}) collective-permute-start(bf16[768,192]{0,1:T(8,128)(2,1)S(1)} %dynamic-slice_bitcast_fusion.4), channel_id=1, source_target_pairs={{0,16},{16,0},{1,17},{17,1},{2,18},{18,2},{3,19},{19,3},{4,20},{20... | collective-permute-start | bytes 884744 | tf_op jit(solution)/shard_map/ppermute | solution.py:455
  555.0 4.7 collective-permute-start.6
  557.3 5.5 collective-permute-start.11
  559.7 4.4 collective-permute-start.7
  562.8 5.2 collective-permute-start.12
  564.1 6.7 %collective-permute-start.8 = (f32[5760]{0:T(1024)S(1)}, f32[5760]{0:T(1024)S(1)}, u32[]{:S(2)}, u32[]{:S(2)}) collective-permute-start(f32[5760]{0:T(1024)S(1)} %add.270), channel_id=1, source_target_pairs={{0,16},{16,0},{1,17},{17,1},{2,18},{18,2},{3,19},{19,3},{4,20},{20... | collective-permute-start | bytes 69128 | tf_op jit(solution)/shard_map/ppermute | solution.py:429
  568.1 4.1 collective-permute-start.13
  (62 other events, 626.4 us)
Sparse Core Ops, SparseCore 0:
  50.4 40.8 all-gather.4
  92.9 22.2 all-gather.8
  143.2 23.4 all-gather.6
  316.0 96.4 all-reduce.2
